TPU v7x, 512 devices: a whole 4x4x16 slice. The times are simulated.
512 devices in a mesh: lat: 16 (over y_hi, x, core), lon: 16 (over z), batch: 2 (over y_lo).
Axes of the slice: x: 4, y: 4 (y_hi: 2, y_lo: 2; y = y_hi * 2 + y_lo), z: 16, core: 2. Of those that a mesh axis runs over, the one named last changes fastest.
Arguments:
- grid: bfloat16 [512, 720, 1440], P('batch', 'lat', 'lon'), parts along dimension 0, may hold values from -6 to 6
- norm_gain: float32 [256], replicated, may hold values from 0.5 to 1.5
- mlp_in: bfloat16 [256, 512], replicated, may hold values from -0.375 to 0.375
- mlp_out: bfloat16 [512, 256], replicated, may hold values from -0.25 to 0.25
- filter_weight: bfloat16 [512, 256, 256], P(('lat', 'lon')), may hold values from -0.375 to 0.375
Outputs:
- updated: bfloat16 [512, 720, 1440], P(('batch', 'lon'), 'lat'), parts along dimension 0
There are 2 independent parts, one for each index of `batch`. A program takes and returns all parts, laid end to end along the dimension named above; an argument that names none is the same for every part. Nothing has to cross between parts.
All inputs are finite; a program needn't handle non-finite values.
Results may differ from a plain program's by a relative error of at most 0.0095.
Values may be sent and summed in bfloat16 or wider, within the bound.
A program may use at most 128 MiB of HBM per device.

v0:
```python
import jax
import jax.numpy as jnp
from jax import lax
from jax.sharding import PartitionSpec as P


def quadrature(nlat):
    rows = jnp.arange(nlat, dtype=jnp.float32)
    theta = jnp.pi * (rows + 0.5) / nlat
    return (theta, jnp.pi / nlat * jnp.sin(theta))


def legendre(orders, nlat, degrees):
    theta = quadrature(nlat)[0]
    cosine = jnp.cos(theta)
    sine = jnp.sin(theta)
    order = orders.astype(jnp.float32)[:, None]
    degree = jnp.arange(degrees, dtype=jnp.float32)[None, :]
    active = degree > order
    second = degree > order + 1.0
    growth = jnp.sqrt(
        jnp.where(active, 4.0 * degree * degree - 1.0, 1.0)
        / jnp.where(active, degree * degree - order * order, 1.0)
    )
    before = degree - 1.0
    damping = jnp.sqrt(
        jnp.where(second, before * before - order * order, 0.0)
        / jnp.where(second, 4.0 * before * before - 1.0, 1.0)
    )
    counts = jnp.arange(1, degrees + 1, dtype=jnp.float32)
    ratios = jnp.log((2.0 * counts - 1.0) / (2.0 * counts))
    partial_log = jnp.sum(jnp.where(counts[None, :] <= order, ratios[None, :], 0.0), axis=1)
    start_log = (
        order * jnp.log(sine)[None, :] + 0.5 * jnp.log(order + 0.5) + 0.5 * partial_log[:, None]
    )

    def advance(carry, inputs):
        upper, lower, scale_log = carry
        grow, damp, live = inputs
        fresh = grow[:, None] * cosine[None, :] * upper - (grow * damp)[:, None] * lower
        largest = jnp.maximum(jnp.abs(fresh), jnp.abs(upper))
        largest = jnp.where(largest > 0.0, largest, 1.0)
        alive = live[:, None]
        new_upper = jnp.where(alive, fresh / largest, upper)
        new_lower = jnp.where(alive, upper / largest, lower)
        new_log = jnp.where(alive, scale_log + jnp.log(largest), scale_log)
        return ((new_upper, new_lower, new_log), new_upper * jnp.exp(new_log + start_log))

    group = 64
    members = orders.shape[0]

    def advance_group(carry, inputs):
        grows, damps, lives = inputs
        outputs = []
        for offset in range(group):
            carry, fresh_row = advance(carry, (grows[offset], damps[offset], lives[offset]))
            outputs.append(fresh_row)
        return (carry, jnp.stack(outputs, axis=0))

    shape = (members, nlat)
    start = (
        jnp.ones(shape, jnp.float32),
        jnp.zeros(shape, jnp.float32),
        jnp.zeros(shape, jnp.float32),
    )
    grouped = (
        growth.T.reshape(degrees // group, group, members),
        damping.T.reshape(degrees // group, group, members),
        active.T.reshape(degrees // group, group, members),
    )
    values = lax.scan(advance_group, start, grouped)[1].reshape(degrees, members, nlat)
    values = values.transpose(1, 0, 2)
    return jnp.where((degree >= order)[:, :, None], values, 0.0)


def forward_table(orders, nlon):
    points = jnp.arange(nlon, dtype=jnp.int32)
    phase = points[:, None] * orders[None, :] % nlon
    angle = 2.0 * jnp.pi / nlon * phase.astype(jnp.float32)
    return jnp.stack([jnp.cos(angle), -jnp.sin(angle)], axis=2).astype(jnp.bfloat16)


def inverse_half(orders, nlon):
    points = jnp.arange(nlon // 2, dtype=jnp.int32)
    phase = orders[:, None] * points[None, :] % nlon
    angle = 2.0 * jnp.pi / nlon * phase.astype(jnp.float32)
    amplitude = jnp.where(orders == 0, 1.0, 2.0).astype(jnp.float32)[:, None]
    return jnp.stack([amplitude * jnp.cos(angle), -amplitude * jnp.sin(angle)], axis=1).astype(
        jnp.bfloat16
    )


def mlp_rows(fields, norm_gain, mlp_in, mlp_out):
    values = fields.astype(jnp.float32)
    mean = jnp.mean(values, axis=0)
    centered = values - mean
    spread = jnp.mean(centered * centered, axis=0)
    normed = (centered * lax.rsqrt(spread + 1e-05) * norm_gain[:, None, None]).astype(jnp.bfloat16)
    flat = normed.reshape(normed.shape[0], -1)
    hidden = jax.nn.gelu(
        jnp.einsum("ch,cp->hp", mlp_in, flat, preferred_element_type=jnp.float32)
    ).astype(jnp.bfloat16)
    update = jnp.einsum("hc,hp->cp", mlp_out, hidden, preferred_element_type=jnp.float32)
    return (values + update.reshape(values.shape)).astype(jnp.bfloat16)


def wave_table(devices):
    device_ids = jnp.arange(devices, dtype=jnp.int32)
    return jnp.stack([2 * device_ids, 2 * device_ids + 1], axis=1)


def analysis_sum(table, fields):
    return jnp.einsum("tlj,tkj->tlk", table, fields, preferred_element_type=jnp.float32)


def synthesis_sum(table, filtered):
    return jnp.einsum("tlj,tlk->tkj", table, filtered, preferred_element_type=jnp.float32)


def on_device(grid, norm_gain, mlp_in, mlp_out, filter_weight):
    width, lat_rows, lon_cols = grid.shape
    n_lat = lax.axis_size("lat")
    n_lon = lax.axis_size("lon")
    devices = n_lat * n_lon
    modes = 2 * devices
    nlat = lat_rows * n_lat
    nlon = lon_cols * n_lon
    mixed = mlp_rows(grid, norm_gain, mlp_in, mlp_out)
    rows = lax.all_to_all(mixed, "lon", split_axis=0, concat_axis=2, tiled=True)
    mode_table = wave_table(devices)
    dft_table = forward_table(mode_table.reshape(-1), nlon).reshape(nlon, 4 * devices)
    spectrum = (
        jnp.einsum("nk,cjn->kcj", dft_table, rows, preferred_element_type=jnp.float32) / nlon
    ).astype(jnp.bfloat16)
    owned = lax.all_to_all(
        lax.all_to_all(spectrum, "lat", split_axis=0, concat_axis=2, tiled=True),
        "lon",
        split_axis=0,
        concat_axis=1,
        tiled=True,
    )
    fields = owned.reshape(2, 2 * width, nlat)
    self_index = lax.axis_index("lat") * n_lon + lax.axis_index("lon")
    device_ids = jnp.arange(devices, dtype=jnp.int32)
    own_modes = jnp.sum(jnp.where(device_ids[:, None] == self_index, mode_table, 0), axis=0)
    table = legendre(own_modes, nlat, modes)
    weights = quadrature(nlat)[1]
    analysis_table = (table * weights).astype(jnp.bfloat16)
    synthesis_table = table.astype(jnp.bfloat16)
    coefficients = analysis_sum(analysis_table, fields).astype(jnp.bfloat16)
    at_owner = lax.all_to_all(
        lax.all_to_all(coefficients, "lat", split_axis=1, concat_axis=0, tiled=True),
        "lon",
        split_axis=1,
        concat_axis=0,
        tiled=True,
    )
    split_parts = at_owner.reshape(at_owner.shape[0], at_owner.shape[1], 2, width)
    filtered = jnp.einsum(
        "slrc,lco->slro", split_parts, filter_weight, preferred_element_type=jnp.float32
    ).astype(jnp.bfloat16)
    outgoing = filtered.reshape(n_lon, n_lat, 2, 1, 1, 2, 2 * width)
    returned = lax.all_to_all(
        lax.all_to_all(outgoing, "lat", split_axis=1, concat_axis=3, tiled=True),
        "lon",
        split_axis=0,
        concat_axis=4,
        tiled=True,
    )
    degree_rows = returned.reshape(2, modes, 2 * width)
    synthesis = synthesis_sum(synthesis_table, degree_rows).astype(jnp.bfloat16)
    spread_out = synthesis.reshape(1, 1, 4, width, nlat)
    gathered_rows = lax.all_to_all(
        lax.all_to_all(spread_out, "lat", split_axis=4, concat_axis=0, tiled=True),
        "lon",
        split_axis=3,
        concat_axis=1,
        tiled=True,
    )
    by_device = gathered_rows.reshape(devices, 2, 2, gathered_rows.shape[3], lat_rows)
    first_even = mode_table[:, 0] % 2 == 0
    pick = first_even[:, None, None, None]
    even_part = jnp.where(pick, by_device[:, 0], by_device[:, 1])
    odd_part = jnp.where(pick, by_device[:, 1], by_device[:, 0])
    even_modes = jnp.where(first_even, mode_table[:, 0], mode_table[:, 1])
    odd_modes = jnp.where(first_even, mode_table[:, 1], mode_table[:, 0])
    evens = jnp.einsum(
        "drn,drcj->cjn",
        inverse_half(even_modes, nlon),
        even_part,
        preferred_element_type=jnp.float32,
    )
    odds = jnp.einsum(
        "drn,drcj->cjn", inverse_half(odd_modes, nlon), odd_part, preferred_element_type=jnp.float32
    )
    spatial = jnp.concatenate([evens + odds, evens - odds], axis=2)
    return (rows.astype(jnp.float32) + spatial).astype(jnp.bfloat16)


def solution(mesh):
    return jax.shard_map(
        on_device,
        mesh=mesh,
        in_specs=(P("batch", "lat", "lon"), P(), P(), P(), P(("lat", "lon"), None, None)),
        out_specs=P(("batch", "lon"), "lat", None),
        check_vma=False,
    )
```

profile of v0, /device:TPU:1, one launch (start us, length us, event | category | flops | bytes accessed | tf_op | source)
XLA Modules:
  0.0 733.8 jit_solution(1430474192069932173)
XLA Ops:
  14.0 6.7 convolution_bitcast_fusion
  25.7 6.3 copy.163
  37.1 15.9 %all-to-all-start = ((bf16[256,45,90]{2,1,0:T(8,128)(2,1)}), bf16[256,45,90]{2,1,0:T(8,128)(2,1)S(1)}, u32[]{:S(2)}, u32[]{:S(2)}) async-start(bf16[256,45,90]{2,1,0:T(8,128)(2,1)} %fusion.273), calls=%async_computation | async-start | bytes 6291456 | tf_op jit(solution)/shard_map/all_to_all | solution.py:129
  53.5 12.7 %cosine_convert_fusion = (bf16[1440,512,1]{1,0,2:T(8,128)(2,1)S(1)}, bf16[1440,512,1]{1,0,2:T(8,128)(2,1)S(1)}) fusion(s32[512]{0:T(512)S(1)} %mul.2740), kind=kLoop, calls=%fused_computation.869 | loop fusion | flops 8847360 | bytes 2951168 | tf_op jit(solution)/shard_map/convert.4
  68.0 8.8 %copy.168 = bf16[1440,512,2]{0,2,1:T(2,128)(2,1)} copy(bf16[1440,512,2]{1,0,2:T(8,128)(2,1)} %pad_maximum_fusion) | data formatting | bytes 5898240 | tf_op jit(solution)/shard_map/stack | solution.py:80
  76.9 7.5 %convert_element_type.122 = bf16[1440,1024]{0,1:T(8,128)(2,1)} reshape(bf16[1440,512,2]{0,2,1:T(2,128)(2,1)} %copy.168) | data formatting | bytes 5898240 | tf_op jit(solution)/shard_map/convert_element_type | solution.py:80
  84.4 105.5 %all-to-all-done = bf16[256,45,90]{2,1,0:T(8,128)(2,1)S(1)} async-done(((bf16[256,45,90]{2,1,0:T(8,128)(2,1)}), bf16[256,45,90]{2,1,0:T(8,128)(2,1)S(1)}, u32[]{:S(2)}, u32[]{:S(2)}) %all-to-all-start) | async-done | bytes 2073632 | tf_op jit(solution)/shard_map/all_to_all | solution.py:129
  198.4 6.7 multiply_convert_fusion
  211.2 10.2 %reshape.1790 = bf16[16,2,23040]{2,1,0:T(2,128)(2,1)} reshape(bf16[1024,16,45]{2,1,0:T(8,128)(2,1)} %copy.171) | data formatting | bytes 2949120
  221.4 11.0 %all-to-all-start.1 = ((bf16[16,2,23040]{2,1,0:T(2,128)(2,1)}), bf16[16,2,23040]{2,1,0:T(2,128)(2,1)S(1)}, u32[]{:S(2)}, u32[]{:S(2)}) async-start(bf16[16,2,23040]{2,1,0:T(2,128)(2,1)} %reshape.1790), calls=%async_computation.1 | async-start | bytes 2949120 | tf_op jit(solution)/shard_map/all_to_all | solution.py:136
  234.0 20.3 %all-to-all-done.1 = bf16[16,2,23040]{2,1,0:T(2,128)(2,1)S(1)} async-done(((bf16[16,2,23040]{2,1,0:T(2,128)(2,1)}), bf16[16,2,23040]{2,1,0:T(2,128)(2,1)S(1)}, u32[]{:S(2)}, u32[]{:S(2)}) %all-to-all-start.1) | async-done | bytes 1474592 | tf_op jit(solution)/shard_map/all_to_all | solution.py:136
  254.3 13.1 %reshape.1791 = bf16[1024,16,45]{2,1,0:T(8,128)(2,1)} reshape(bf16[16,2,23040]{2,1,0:T(2,128)(2,1)S(1)} %all-to-all-done.1) | data formatting | bytes 2949120
  267.4 8.0 %copy.173 = bf16[64,16,16,45]{0,1,3,2:T(8,128)(2,1)S(1)} copy(bf16[64,16,16,45]{3,1,0,2:T(8,128)(2,1)} %bitcast.996) | data formatting | bytes 2949120 | tf_op jit(solution)/shard_map/all_to_all | solution.py:136
  280.6 8.2 %all-to-all-start.2 = ((bf16[64,16,720]{2,1,0:T(8,128)(2,1)}), bf16[64,16,720]{2,1,0:T(8,128)(2,1)}, u32[]{:S(2)}, u32[]{:S(2)}) async-start(bf16[64,16,720]{2,1,0:T(8,128)(2,1)} %copy.174), calls=%async_computation.2 | async-start | bytes 3145728 | tf_op jit(solution)/shard_map/all_to_all | solution.py:135
  288.8 104.5 %while.18 = (s32[]{:T(128)}, f32[2,720]{1,0:T(2,128)S(1)}, f32[2,720]{1,0:T(2,128)S(1)}, f32[2,720]{1,0:T(2,128)S(1)}, f32[8,64,2,720]{3,2,1,0:T(2,128)}, /*inde...) while((s32[]{:T(128)}, f32[2,720]{1,0:T(2,128)S(1)}, ...), condition=%wide.region_5.6_spmd.clone.clone, body=%wide.region_4.5_spmd.clone.clone.sunk | while | flops 1948513 | bytes 5262132 | solution.py:71
  401.6 20.9 %all_to_all.150 = bf16[2,512,512]{2,0,1:T(2,128)(2,1)S(1)} all-to-all(bf16[2,512,512]{2,0,1:T(2,128)(2,1)S(1)} %copy.177), channel_id=1, replica_groups=mesh['lat'=16,'lon'=16,'batch'=2] {'lat'}, dimensions={1} | all-to-all | bytes 2097152 | tf_op jit(solution)/shard_map/all_to_all | solution.py:152
  423.4 57.1 %all_to_all.151 = bf16[32,32,512]{2,0,1:T(8,128)(2,1)S(1)} all-to-all(bf16[32,32,512]{2,0,1:T(8,128)(2,1)S(1)} %copy.180), channel_id=1, replica_groups=mesh['lat'=16,'lon'=16,'batch'=2] {'lon'}, dimensions={1} | all-to-all | bytes 2097152 | tf_op jit(solution)/shard_map/all_to_all | solution.py:151
  493.8 27.1 %all_to_all.152 = bf16[16,16,2,1,1,2,512]{6,5,2,0,4,3,1:T(2,128)(2,1)S(1)} all-to-all(bf16[16,16,2,1,1,2,512]{6,5,2,0,4,3,1:T(2,128)(2,1)S(1)} %copy.184), channel_id=1, replica_groups=mesh['lat'=16,'lon'=16,'batch'=2] {'lat'}, dimensions={1} | all-to-all | bytes 2097152 | tf_op jit(solution)/shard_map/all_to_all | solution.py:164
  521.9 51.2 %all_to_all.153 = bf16[16,1,2,16,1,2,512]{6,5,2,3,4,1,0:T(2,128)(2,1)S(1)} all-to-all(bf16[16,1,2,16,1,2,512]{6,5,2,3,4,1,0:T(2,128)(2,1)S(1)} %copy.185), channel_id=1, replica_groups=mesh['lat'=16,'lon'=16,'batch'=2] {'lon'}, dimensions={0} | all-to-all | bytes 2097152 | tf_op jit(solution)/shard_map/all_to_all | solution.py:163
  583.7 31.5 %all_to_all.154 = bf16[1,1,4,256,720]{3,2,1,0,4:T(4,128)(2,1)S(1)} all-to-all(bf16[1,1,4,256,720]{3,2,1,0,4:T(4,128)(2,1)S(1)} %copy.188), channel_id=1, replica_groups=mesh['lat'=16,'lon'=16,'batch'=2] {'lat'}, dimensions={4} | all-to-all | bytes 2949120 | tf_op jit(solution)/shard_map/all_to_all | solution.py:174
  615.1 7.4 %copy.189 = bf16[16,1,4,256,45]{4,0,2,1,3:T(8,128)(2,1)} copy(bf16[16,1,4,256,45]{3,2,4,0,1:T(4,128)(2,1)S(1)} %bitcast.1004) | data formatting | bytes 2949120 | tf_op jit(solution)/shard_map/all_to_all | solution.py:174
  622.5 10.2 %reshape.1792 = bf16[16,2,23040]{2,1,0:T(2,128)(2,1)} reshape(bf16[256,1,4,16,45]{4,3,2,1,0:T(8,128)(2,1)} %bitcast.998) | data formatting | bytes 2949120
  645.8 58.0 %all-to-all-done.8 = bf16[16,2,23040]{2,1,0:T(2,128)(2,1)S(1)} async-done(((bf16[16,2,23040]{2,1,0:T(2,128)(2,1)}), bf16[16,2,23040]{2,1,0:T(2,128)(2,1)S(1)}, u32[]{:S(2)}, u32[]{:S(2)}) %all-to-all-start.8) | async-done | bytes 1474592 | tf_op jit(solution)/shard_map/all_to_all | solution.py:173
  703.8 13.1 %reshape.1793 = bf16[256,1,4,16,45]{4,3,2,1,0:T(8,128)(2,1)} reshape(bf16[16,2,23040]{2,1,0:T(2,128)(2,1)S(1)} %all-to-all-done.8) | data formatting | bytes 2949120
  (699 shorter events, 215.2 us)
Async XLA Ops:
  0.0 14.0 %copy-start = (bf16[512,256]{1,0:T(8,128)(2,1)S(1)}, bf16[512,256]{1,0:T(8,128)(2,1)}, u32[]{:S(2)}) copy-start(bf16[512,256]{1,0:T(8,128)(2,1)} %param.10) | copy-start | bytes 786436
  3.6 1.8 copy-start.5
  37.1 152.7 %all-to-all-start = ((bf16[256,45,90]{2,1,0:T(8,128)(2,1)}), bf16[256,45,90]{2,1,0:T(8,128)(2,1)S(1)}, u32[]{:S(2)}, u32[]{:S(2)}) async-start(bf16[256,45,90]{2,1,0:T(8,128)(2,1)} %fusion.273), calls=%async_computation | async-start | bytes 6291456 | tf_op jit(solution)/shard_map/all_to_all | solution.py:129
  198.4 6.7 copy-start.2
  221.4 32.8 %all-to-all-start.1 = ((bf16[16,2,23040]{2,1,0:T(2,128)(2,1)}), bf16[16,2,23040]{2,1,0:T(2,128)(2,1)S(1)}, u32[]{:S(2)}, u32[]{:S(2)}) async-start(bf16[16,2,23040]{2,1,0:T(2,128)(2,1)} %reshape.1790), calls=%async_computation.1 | async-start | bytes 2949120 | tf_op jit(solution)/shard_map/all_to_all | solution.py:136
  280.6 117.0 %all-to-all-start.2 = ((bf16[64,16,720]{2,1,0:T(8,128)(2,1)}), bf16[64,16,720]{2,1,0:T(8,128)(2,1)}, u32[]{:S(2)}, u32[]{:S(2)}) async-start(bf16[64,16,720]{2,1,0:T(8,128)(2,1)} %copy.174), calls=%async_computation.2 | async-start | bytes 3145728 | tf_op jit(solution)/shard_map/all_to_all | solution.py:135
  423.4 60.3 %copy-start.4 = (bf16[2,256,256]{2,1,0:T(8,128)(2,1)S(1)}, bf16[2,256,256]{2,1,0:T(8,128)(2,1)}, u32[]{:S(2)}) copy-start(bf16[2,256,256]{2,1,0:T(8,128)(2,1)} %param.11) | copy-start | bytes 786436
  632.7 71.0 %all-to-all-start.8 = ((bf16[16,2,23040]{2,1,0:T(2,128)(2,1)}), bf16[16,2,23040]{2,1,0:T(2,128)(2,1)S(1)}, u32[]{:S(2)}, u32[]{:S(2)}) async-start(bf16[16,2,23040]{2,1,0:T(2,128)(2,1)} %reshape.1792), calls=%async_computation.8 | async-start | bytes 2949120 | tf_op jit(solution)/shard_map/all_to_all | solution.py:173
  728.7 2.5 copy-start.3
  731.1 2.4 copy-start.1
where the time goes:
time: 748 us; the launch traced here: 734 us
  blocking collectives  188 us (25%)
  waiting for transfers between devices  184 us (25%)
  local copies, waits for them, and re-layouts  163 us (22%)
  other arithmetic  132 us (18%)
  starting transfers between devices  41.3 us (6%)
  matrix products  24.2 us (3%)
    all_to_all x1, waiting for transfers between devices, on_device(): rows = lax.all_to_all(mixed, 'lon', split_axis=0, concat_axis=2, tiled=True)  105 us
    all_to_all x1, waiting for transfers between devices, on_device(): lax.all_to_all(lax.all_to_all(spread_out, 'lat', split_axis=4, concat_axi...  58 us
    all_to_all x1, blocking collectives, on_device(): lax.all_to_all(lax.all_to_all(coefficients, 'lat', split_axis=1, concat_a...  57.1 us
    while x504, other arithmetic  55.3 us
    all_to_all x1, blocking collectives, on_device(): lax.all_to_all(lax.all_to_all(outgoing, 'lat', split_axis=1, concat_axis=...  51.2 us
    unnamed x17, local copies, waits for them, and re-layouts  50.2 us
    mul x32, other arithmetic, advance(): grow * damp  36.6 us
    all_to_all x1, blocking collectives, on_device(): lax.all_to_all(spread_out, 'lat', split_axis=4, concat_axis=0, tiled=True)  31.5 us
  transfers between devices with their start and end apart: 4, of which 3 were waited for; matrix products, arithmetic and copies ran while one was open for 20% of the time, Pallas kernels for 0%

commit v1 on v0

v1 whole, which is shorter than its diff:
```python
import functools

import jax
import jax.numpy as jnp
from jax import lax
from jax.experimental import pallas as pl
from jax.experimental.pallas import tpu as pltpu
from jax.sharding import PartitionSpec as P

F32 = jnp.float32
BF16 = jnp.bfloat16

CH = 256
HID = 512
JD = 45
JP = 48
ND = 90
NP = 96
NLAT = 720
NLON = 1440
MODES = 512
NA = 16
NZ = 16
JALL = NA * JP
ROWS = 144
LIMIT = 56 * 1024 * 1024


def call(kernel, out_shape, grid, in_specs, out_specs, scratch, flops, moved):
    return pl.pallas_call(
        kernel,
        out_shape=out_shape,
        grid=grid,
        in_specs=in_specs,
        out_specs=out_specs,
        scratch_shapes=scratch,
        cost_estimate=pl.CostEstimate(flops=flops, bytes_accessed=moved, transcendentals=0),
        compiler_params=pltpu.CompilerParams(
            dimension_semantics=("arbitrary",) * len(grid), vmem_limit_bytes=LIMIT
        ),
    )


def swap_blocks(xs):
    block = lax.broadcasted_iota(jnp.int32, xs[0].shape, 1) // 16
    for bit in (1, 2, 4):
        upper = (block & bit) != 0
        new = list(xs)
        for i in range(8):
            if i & bit == 0:
                low, high = xs[i], xs[i | bit]
                new[i] = jnp.where(upper, pltpu.roll(high, 16 * bit, 1), low)
                new[i | bit] = jnp.where(upper, high, pltpu.roll(low, 128 - 16 * bit, 1))
        xs = new
    return xs


def mlp_kernel(x_ref, gain_ref, in_ref, out_w_ref, o_ref, pad_ref, mix_ref):
    g = pl.program_id(0)
    pad_ref[...] = jnp.zeros_like(pad_ref)
    for j in range(8):
        pad_ref[j * NP : j * NP + ND, :] = x_ref[j].astype(F32)
    half = 2 * NP
    for part in range(4):
        rows = slice(part * half, (part + 1) * half)
        x = pad_ref[rows, :]
        mean = jnp.mean(x, axis=1, keepdims=True)
        centered = x - mean
        spread = jnp.mean(centered * centered, axis=1, keepdims=True)
        normed = (centered * lax.rsqrt(spread + 1e-05) * gain_ref[...]).astype(BF16)
        hidden = jnp.dot(normed, in_ref[...], preferred_element_type=F32)
        hidden = jax.nn.gelu(hidden).astype(BF16)
        mixed = x + jnp.dot(hidden, out_w_ref[...], preferred_element_type=F32)
        mix_ref[0, rows, :] = mixed[:, :128]
        mix_ref[1, rows, :] = mixed[:, 128:]
    lane = lax.broadcasted_iota(jnp.int32, (16, 128), 1)
    row = lax.broadcasted_iota(jnp.int32, (16, 128), 0)
    live = lane // 16 < JD - 8 * g

    def place(step, _):
        start = pl.multiple_of(step * 16, 16)
        keep = jnp.logical_and(live, row < ND - start)
        for h in range(2):
            xs = [mix_ref[h, pl.ds(pl.multiple_of(j * NP + start, 16), 16), :] for j in range(8)]
            for z, y in enumerate(swap_blocks(xs)):
                o_ref[h * 8 + z, 0, pl.ds(start, 16), :] = jnp.where(keep, y, 0.0).astype(BF16)
        return 0

    lax.fori_loop(0, NP // 16, place, 0)


def mlp(points, gain, mlp_in, mlp_out):
    return call(
        mlp_kernel,
        jax.ShapeDtypeStruct((NZ, 6, NP, 128), BF16),
        (6,),
        [
            pl.BlockSpec((8, ND, CH), lambda g: (g, 0, 0)),
            pl.BlockSpec((1, CH), lambda g: (0, 0)),
            pl.BlockSpec((CH, HID), lambda g: (0, 0)),
            pl.BlockSpec((HID, CH), lambda g: (0, 0)),
        ],
        pl.BlockSpec((NZ, 1, NP, 128), lambda g: (0, g, 0, 0)),
        [pltpu.VMEM((8 * NP, CH), F32), pltpu.VMEM((2, 8 * NP, 128), F32)],
        4 * 4050 * CH * HID,
        5_000_000,
    )(points, gain, mlp_in, mlp_out)


def dft_kernel(x_ref, table_ref, weight_ref, o_ref, acc_ref, swap_ref):
    both = jnp.concatenate(
        [x_ref[:, gg].reshape(NZ * NP, 128) for gg in range(2)], axis=1
    )
    for part in range(4):
        rows = slice(part * 256, (part + 1) * 256)
        acc = jnp.dot(table_ref[rows, :], both, preferred_element_type=F32)
        acc = acc * weight_ref[0]
        acc_ref[0, rows, :] = acc[:, :128]
        acc_ref[1, rows, :] = acc[:, 128:]

    def place(a, _):
        for gg in range(2):
            xs = [
                acc_ref[gg, pl.ds(pl.multiple_of(a * 64 + mr * 8, 8), 8), :] for mr in range(8)
            ]
            for j, y in enumerate(swap_blocks(xs)):
                swap_ref[pl.ds(gg * 8 + j, 8, stride=16), :] = y
        o_ref[a] = swap_ref[...].astype(BF16).reshape(8, 16, 128)
        return 0

    lax.fori_loop(0, NA, place, 0)


def dft(fields, table, weights):
    return call(
        dft_kernel,
        jax.ShapeDtypeStruct((NA, 8, JP, 128), BF16),
        (3,),
        [
            pl.BlockSpec((NZ, 2, NP, 128), lambda g: (0, g, 0, 0)),
            pl.BlockSpec((2 * MODES, NZ * NP), lambda g: (0, 0)),
            pl.BlockSpec((1, 1, 256), lambda g: (g, 0, 0)),
        ],
        pl.BlockSpec((NA, 8, 16, 128), lambda g: (0, 0, g, 0)),
        [pltpu.VMEM((2, 2 * MODES, 128), F32), pltpu.VMEM((128, 128), F32)],
        2 * 2 * MODES * NZ * NP * JALL,
        7_000_000,
    )(fields, table, weights)


def legendre_kernel(order_ref, cos_ref, log_ref, o_ref, up_ref, low_ref, scale_ref, swap_ref):
    q = pl.program_id(0)
    lb = pl.program_id(1)

    @pl.when(lb == 0)
    def _():
        up_ref[...] = jnp.zeros_like(up_ref)
        low_ref[...] = jnp.zeros_like(low_ref)
        scale_ref[...] = log_ref[0]

    @pl.when(lb >= q)
    def _():
        order = order_ref[0]
        degree = lax.broadcasted_iota(jnp.int32, (8, 128), 1).astype(F32) + (lb * 128).astype(F32)
        active = degree > order
        second = degree > order + 1.0
        grow = jnp.sqrt(
            jnp.where(active, 4.0 * degree * degree - 1.0, 0.0)
            / jnp.where(active, degree * degree - order * order, 1.0)
        )
        before = degree - 1.0
        damp = jnp.sqrt(
            jnp.where(second, before * before - order * order, 0.0)
            / jnp.where(second, 4.0 * before * before - 1.0, 1.0)
        )
        damp = grow * damp
        first = jnp.where(degree == order, 1.0, 0.0)

        def group(i, _):
            shift = lax.rem(128 - 16 * i, 128)
            grow_i = pltpu.roll(grow, shift, 1)
            damp_i = pltpu.roll(damp, shift, 1)
            first_i = pltpu.roll(first, shift, 1)
            for k in range(6):
                cols = slice(k * 128, (k + 1) * 128)
                up = up_ref[:, cols]
                low = low_ref[:, cols]
                scale_log = scale_ref[:, cols]
                root = jnp.exp(0.5 * scale_log)
                cosine = cos_ref[:, cols]
                for s in range(16):
                    a = jnp.broadcast_to(grow_i[:, s : s + 1], (8, 128))
                    b = jnp.broadcast_to(damp_i[:, s : s + 1], (8, 128))
                    e = jnp.broadcast_to(first_i[:, s : s + 1], (8, 128))
                    fresh = a * (cosine * up) - b * low + e
                    low = up
                    up = fresh
                    swap_ref[k, s * 8 : s * 8 + 8, :] = fresh * root * root
                largest = jnp.maximum(jnp.abs(up), jnp.abs(low))
                largest = jnp.where(largest > 0.0, largest, 1.0)
                up_ref[:, cols] = up / largest
                low_ref[:, cols] = low / largest
                scale_ref[:, cols] = scale_log + jnp.log(largest)
            start = pl.multiple_of(i * 16, 16)
            for m in range(8):
                for k in range(6):
                    o_ref[0, 0, m, pl.ds(start, 16), k * 128 : (k + 1) * 128] = swap_ref[
                        k, pl.ds(m, 16, stride=8), :
                    ].astype(BF16)
            return 0

        lax.fori_loop(0, 8, group, 0)


def legendre(orders, cosine, start_log):
    return call(
        legendre_kernel,
        jax.ShapeDtypeStruct((4, 4, 8, 128, JALL), BF16),
        (4, 4),
        [
            pl.BlockSpec((1, 8, 128), lambda q, b: (q, 0, 0)),
            pl.BlockSpec((8, JALL), lambda q, b: (0, 0)),
            pl.BlockSpec((1, 8, JALL), lambda q, b: (q, 0, 0)),
        ],
        pl.BlockSpec((1, 1, 8, 128, JALL), lambda q, b: (q, jnp.maximum(b, q), 0, 0, 0)),
        [
            pltpu.VMEM((8, JALL), F32),
            pltpu.VMEM((8, JALL), F32),
            pltpu.VMEM((8, JALL), F32),
            pltpu.VMEM((6, 128, 128), F32),
        ],
        200_000_000,
        16_000_000,
    )(orders, cosine, start_log)


def analysis_kernel(table_ref, x_ref, o_ref, all_ref):
    q = pl.program_id(0)
    lb = pl.program_id(1)
    block = lax.broadcasted_iota(jnp.int32, (128, 128), 1) // 32

    @pl.when(lb >= q)
    def _():
        for i in range(2):
            x = x_ref[:, i].reshape(JALL, 128)
            total = jnp.zeros((128, 128), F32)
            for m in range(4):
                part = jnp.dot(table_ref[0, 0, i * 4 + m], x, preferred_element_type=F32)
                total = jnp.where(block == m, part, total)
            all_ref[2 * q + i, pl.ds(pl.multiple_of(lb * 128, 128), 128), :] = total

    @pl.when(jnp.logical_and(q == 3, lb == 3))
    def _():
        row = lax.broadcasted_iota(jnp.int32, (16, 128), 0)

        def place(z, _):
            for t in range(2):
                parts = [all_ref[g, pl.ds(2 * z + t, 16, stride=32), :] for g in range(8)]
                o_ref[z, t * 16 : t * 16 + 16, :] = parts[0].astype(BF16)
                for s in range(1, 4):
                    both = jnp.where(row < 2 * s, pltpu.roll(parts[8 - s], 2 * s, 0), parts[s])
                    o_ref[z, s * 32 + t * 16 : s * 32 + t * 16 + 16, :] = both.astype(BF16)
                if t == 0:
                    kept = parts[4][8:]
                else:
                    o_ref[z, 128:144, :] = jnp.concatenate([kept, parts[4][8:]], axis=0).astype(
                        BF16
                    )
            return 0

        lax.fori_loop(0, NZ, place, 0)


def analysis(table, fields):
    return call(
        analysis_kernel,
        jax.ShapeDtypeStruct((NZ, ROWS, 128), BF16),
        (4, 4),
        [
            pl.BlockSpec((1, 1, 8, 128, JALL), lambda q, b: (q, jnp.maximum(b, q), 0, 0, 0)),
            pl.BlockSpec((NA, 2, JP, 128), lambda q, b: (0, q, 0, 0)),
        ],
        pl.BlockSpec((NZ, ROWS, 128), lambda q, b: (0, 0, 0)),
        [pltpu.VMEM((8, MODES, 128), F32)],
        2 * 80 * 128 * JALL * 128,
        18_000_000,
    )(table, fields)


def filter_row(mg, a, t):
    if mg < 4:
        return 32 * mg + 16 * t + a
    if mg == 4:
        return 128 + 8 * t + a - 8
    return 32 * (8 - mg) + 16 * t + a - 2 * mg


def filter_kernel(x_ref, w_ref, o_ref, in_ref, out_ref):
    def gather(step, _):
        start = pl.multiple_of(step * 16, 16)
        for h in range(2):
            xs = [x_ref[h * 8 + z, pl.ds(start, 16), :].astype(F32) for z in range(8)]
            for mr, y in enumerate(swap_blocks(xs)):
                in_ref[h, pl.ds(start * 8 + mr, 16, stride=8), :] = y
        return 0

    lax.fori_loop(0, ROWS // 16, gather, 0)
    for a in range(16):
        for t in range(2):
            rows = [8 * filter_row(mg, a, t) for mg in range(a // 2 + 1)]
            x = jnp.concatenate(
                [
                    jnp.concatenate([in_ref[h, r : r + 8, :] for r in rows], axis=0)
                    for h in range(2)
                ],
                axis=1,
            ).astype(BF16)
            y = jnp.dot(x, w_ref[a, t], preferred_element_type=F32)
            for i, r in enumerate(rows):
                for h in range(2):
                    out_ref[h, r : r + 8, :] = y[i * 8 : i * 8 + 8, h * 128 : h * 128 + 128]

    def scatter(step, _):
        start = pl.multiple_of(step * 16, 16)
        for h in range(2):
            xs = [out_ref[h, pl.ds(start * 8 + mr, 16, stride=8), :] for mr in range(8)]
            for z, y in enumerate(swap_blocks(xs)):
                o_ref[h * 8 + z, pl.ds(start, 16), :] = y.astype(BF16)
        return 0

    lax.fori_loop(0, ROWS // 16, scatter, 0)


def channel_filter(coefficients, weight):
    whole = pl.BlockSpec((NZ, ROWS, 128), lambda i: (0, 0, 0))
    return call(
        filter_kernel,
        jax.ShapeDtypeStruct((NZ, ROWS, 128), BF16),
        (1,),
        [whole, pl.BlockSpec((NA, 2, CH, CH), lambda i: (0, 0, 0, 0))],
        whole,
        [pltpu.VMEM((2, ROWS * 8, 128), F32), pltpu.VMEM((2, ROWS * 8, 128), F32)],
        2 * ROWS * 8 * CH * CH,
        6_000_000,
    )(coefficients, weight)


def synthesis_kernel(table_ref, x_ref, o_ref, all_ref, acc_ref):
    q = pl.program_id(0)
    lb = pl.program_id(1)

    @pl.when(jnp.logical_and(q == 0, lb == 0))
    def _():
        row = lax.broadcasted_iota(jnp.int32, (16, 128), 0)

        def place(z, _):
            last = x_ref[z, 128:144, :].astype(F32)
            for t in range(2):
                where = pl.ds(2 * z + t, 16, stride=32)
                all_ref[0, where, :] = x_ref[z, t * 16 : t * 16 + 16, :].astype(F32)
                for s in range(1, 4):
                    x = x_ref[z, s * 32 + t * 16 : s * 32 + t * 16 + 16, :].astype(F32)
                    all_ref[s, where, :] = jnp.where(row >= 2 * s, x, 0.0)
                    all_ref[8 - s, where, :] = jnp.where(
                        row >= 16 - 2 * s, pltpu.roll(x, 16 - 2 * s, 0), 0.0
                    )
                all_ref[4, where, :] = jnp.concatenate(
                    [jnp.zeros((8, 128), F32), last[t * 8 : t * 8 + 8]], axis=0
                )
            return 0

        lax.fori_loop(0, NZ, place, 0)

    @pl.when(lb == 0)
    def _():
        acc_ref[...] = jnp.zeros_like(acc_ref)

    @pl.when(lb >= q)
    def _():
        for i in range(2):
            x = all_ref[2 * q + i, pl.ds(pl.multiple_of(lb * 128, 128), 128), :]
            x = x.T.astype(BF16)
            for m in range(4):
                rows = slice(m * 32, m * 32 + 32)
                acc_ref[i, rows, :] += jnp.dot(
                    x[rows], table_ref[0, 0, i * 4 + m], preferred_element_type=F32
                )

    @pl.when(lb == 3)
    def _():
        for i in range(2):
            o_ref[:, i] = acc_ref[i].T.astype(BF16).reshape(NA, JP, 128)


def synthesis(table, filtered):
    return call(
        synthesis_kernel,
        jax.ShapeDtypeStruct((NA, 8, JP, 128), BF16),
        (4, 4),
        [
            pl.BlockSpec((1, 1, 8, 128, JALL), lambda q, b: (q, jnp.maximum(b, q), 0, 0, 0)),
            pl.BlockSpec((NZ, ROWS, 128), lambda q, b: (0, 0, 0)),
        ],
        pl.BlockSpec((NA, 2, JP, 128), lambda q, b: (0, q, 0, 0)),
        [pltpu.VMEM((8, MODES, 128), F32), pltpu.VMEM((2, 128, JALL), F32)],
        2 * 80 * 128 * JALL * 32,
        18_000_000,
    )(table, filtered)


def inverse_kernel(u_ref, x_ref, table_ref, o_ref, wide_ref, rows_ref, lhs_ref, acc_ref):
    def place(a, _):
        wide_ref[...] = u_ref[a].reshape(128, 128).astype(F32)
        for gg in range(2):
            xs = [wide_ref[pl.ds(gg * 8 + j, 8, stride=16), :] for j in range(8)]
            for mr, y in enumerate(swap_blocks(xs)):
                rows_ref[gg, pl.ds(pl.multiple_of(a * 64 + mr * 8, 8), 8), :] = y
        return 0

    lax.fori_loop(0, NA, place, 0)
    for gg in range(2):
        for k in range(8):
            cols = slice(k * 128, (k + 1) * 128)
            lhs_ref[gg * 128 : gg * 128 + 128, cols] = rows_ref[gg, cols, :].T.astype(BF16)
    for part in range(2):
        rows = slice(part * 128, part * 128 + 128)
        acc_ref[rows, :NLON] = jnp.dot(lhs_ref[rows, :], table_ref[...], preferred_element_type=F32)
    row = lax.broadcasted_iota(jnp.int32, (NP, 256), 0)
    lane = lax.broadcasted_iota(jnp.int32, (NP, 256), 1)
    for z in range(NZ):
        begin = ND * z // 128 * 128
        pick = jnp.logical_and(lane == row + (ND * z - begin), row < ND)
        pick = jnp.where(pick, 1.0, 0.0).astype(BF16)
        for gg in range(2):
            x = x_ref[z, gg].astype(F32).T.astype(BF16)
            acc_ref[gg * 128 : gg * 128 + 128, begin : begin + 256] += jnp.dot(
                x, pick, preferred_element_type=F32
            )
    o_ref[...] = acc_ref[:, :NLON].astype(BF16).reshape(16, 16, NLON)


def inverse(waves, fields, table):
    return call(
        inverse_kernel,
        jax.ShapeDtypeStruct((JD, 16, NLON), BF16),
        (3,),
        [
            pl.BlockSpec((NA, 8, 16, 128), lambda g: (0, 0, g, 0)),
            pl.BlockSpec((NZ, 2, NP, 128), lambda g: (0, g, 0, 0)),
            pl.BlockSpec((2 * MODES, NLON), lambda g: (0, 0)),
        ],
        pl.BlockSpec((16, 16, NLON), lambda g: (g, 0, 0)),
        [
            pltpu.VMEM((128, 128), F32),
            pltpu.VMEM((2, 2 * MODES, 128), F32),
            pltpu.VMEM((256, 2 * MODES), BF16),
            pltpu.VMEM((256, 1536), F32),
        ],
        2 * 2 * MODES * NLON * JALL,
        10_000_000,
    )(waves, fields, table)


def wave_rows():
    row = jnp.arange(2 * MODES, dtype=jnp.int32)
    a, mr, mg = row // 64, row // 8 % 8, row % 8
    return 64 * mg + 32 * (mr // 4) + 2 * a + mr // 2 % 2, mr % 2


def waves(orders, part, points):
    phase = (orders[:, None] * points[None, :] + 360 * part[:, None]) % NLON
    return jnp.cos(2.0 * jnp.pi / NLON * phase.astype(F32))


def forward_table():
    orders, part = wave_rows()
    column = jnp.arange(NZ * NP, dtype=jnp.int32)
    n = column % NP
    table = waves(orders, part, column // NP * ND + n)
    return jnp.where(n[None, :] < ND, table, 0.0).astype(BF16)


def inverse_table():
    orders, part = wave_rows()
    table = waves(orders, part, jnp.arange(NLON, dtype=jnp.int32))
    amplitude = jnp.where(orders == 0, 1.0, 2.0).astype(F32)
    return (table * amplitude[:, None]).astype(BF16)


def legendre_inputs(lat_index):
    slot = jnp.arange(32, dtype=jnp.int32)
    orders = (32 * (slot // 2) + 2 * lat_index + slot % 2).astype(F32)
    column = jnp.arange(JALL, dtype=jnp.int32)
    local = column % JP
    theta = jnp.pi * ((column // JP * JD + local).astype(F32) + 0.5) / NLAT
    real = local < JD
    cosine = jnp.where(real, jnp.cos(theta), 0.0)
    log_sine = jnp.log(jnp.where(real, jnp.sin(theta), 1.0))
    counts = jnp.arange(1, MODES + 1, dtype=F32)
    ratios = jnp.log((2.0 * counts - 1.0) / (2.0 * counts))
    partial_log = jnp.sum(jnp.where(counts[None, :] <= orders[:, None], ratios[None, :], 0.0), axis=1)
    start_log = (
        orders[:, None] * log_sine[None, :]
        + 0.5 * jnp.log(orders + 0.5)[:, None]
        + 0.5 * partial_log[:, None]
    )
    start_log = jnp.where(real[None, :], start_log, -1e9)
    return (
        jnp.broadcast_to(orders.reshape(4, 8, 1), (4, 8, 128)),
        jnp.broadcast_to(cosine[None, :], (8, JALL)),
        start_log.reshape(4, 8, JALL),
    )


def spectrum_weights(lat_index):
    lane = jnp.arange(6 * 128, dtype=jnp.int32)
    local = lane // 16
    theta = jnp.pi * ((lat_index * JD + local).astype(F32) + 0.5) / NLAT
    weights = jnp.pi / NLAT * jnp.sin(theta) / NLON
    return jnp.where(local < JD, weights, 0.0).reshape(3, 1, 256)


def exchange(x, axis):
    return lax.all_to_all(x, axis, split_axis=0, concat_axis=0, tiled=True)


def on_device(grid, norm_gain, mlp_in, mlp_out, filter_weight):
    lat_index = lax.axis_index("lat")
    points = grid.transpose(1, 2, 0)
    mixed = mlp(points, norm_gain.reshape(1, CH), mlp_in, mlp_out)
    weight = lax.all_gather(filter_weight, "lat")
    rows = exchange(mixed, "lon")
    table = legendre(*legendre_inputs(lat_index))
    spectrum = dft(rows, forward_table(), spectrum_weights(lat_index))
    coefficients = analysis(table, exchange(spectrum, "lat"))
    filtered = channel_filter(exchange(coefficients, "lon"), weight)
    synthesized = synthesis(table, exchange(filtered, "lon"))
    updated = inverse(exchange(synthesized, "lat"), rows, inverse_table())
    return updated.transpose(1, 0, 2)


def solution(mesh):
    return jax.shard_map(
        on_device,
        mesh=mesh,
        in_specs=(P("batch", "lat", "lon"), P(), P(), P(), P(("lat", "lon"), None, None)),
        out_specs=P(("batch", "lon"), "lat", None),
        check_vma=False,
    )
```

time: 748 us -> 390 us (0.52); the launches traced: 734 us -> 389 us
  local copies, waits for them, and re-layouts: 163 us -> 5.84 us
  blocking collectives: 188 us -> 45.6 us
  Pallas kernels: 0 us -> 123 us
  waiting for transfers between devices: 184 us -> 102 us
  other arithmetic: 132 us -> 56.2 us
  matrix products: 24.2 us -> 0 us
  between operations: 0.66 us -> 13.5 us
    all_to_all x5 -> x1, blocking collectives: 188 us -> 45.6 us  [exchange(): return lax.all_to_all(x, axis, split_axis=0, concat_axis=0, tiled=True)]
    pallas_call x0 -> x7, Pallas kernels: none -> 123 us  [the longest x1 31 us: legendre(): call(legendre_kernel, jax.ShapeDtypeStruct((4, 4, 8, 128, JALL), BF16), (...]
    all_to_all x4, waiting for transfers between devices: 184 us -> 101 us  [exchange(): return lax.all_to_all(x, axis, split_axis=0, concat_axis=0, tiled=True)]
    while x504 -> x0, other arithmetic: 55.3 us -> none
    unnamed x17 -> x8, local copies, waits for them, and re-layouts: 50.2 us -> 4.5 us
    convert_element_type x4, other arithmetic: 10.2 us -> 54.3 us  [the longest x1 27.6 us: inverse_table(): return (table * amplitude[:, None]).astype(BF16)]
    all_to_all x14 -> x0, local copies, waits for them, and re-layouts: 41.7 us -> none  [the longest x2 13.2 us: on_device(): lax.all_to_all(spectrum, 'lat', split_axis=0, concat_axis=2, tiled=True)]
    mul x37 -> x2, other arithmetic: 36.7 us -> 0.02 us  [the longest x1 0.02 us: legendre_inputs(): 0.5 * jnp.log(orders + 0.5)[:, None]]
  transfers between devices with their start and end apart: 4 -> 5, of which waited for: 3 -> 2; matrix products, arithmetic and copies ran while one was open for 20% -> 15% of each run, Pallas kernels for 0% -> 16%
where the time goes in v1:
time: 390 us; the launch traced here: 389 us
  Pallas kernels  123 us (32%)
  waiting for transfers between devices  102 us (26%)
  other arithmetic  56.2 us (14%)
  blocking collectives  45.6 us (12%)
  starting transfers between devices  43.8 us (11%)
  between operations  13.5 us (3%)
  local copies, waits for them, and re-layouts  5.84 us (1%)
    all_to_all x4, waiting for transfers between devices, exchange(): return lax.all_to_all(x, axis, split_axis=0, concat_axis=0, tiled=True)  101 us
    all_to_all x1, blocking collectives, exchange(): return lax.all_to_all(x, axis, split_axis=0, concat_axis=0, tiled=True)  45.6 us
    all_to_all x4, starting transfers between devices, exchange(): return lax.all_to_all(x, axis, split_axis=0, concat_axis=0, tiled=True)  43.7 us
    pallas_call x1, Pallas kernels, legendre(): call(legendre_kernel, jax.ShapeDtypeStruct((4, 4, 8, 128, JALL), BF16), (...  31 us
    convert_element_type x1, other arithmetic, inverse_table(): return (table * amplitude[:, None]).astype(BF16)  27.6 us
    convert_element_type x1, other arithmetic, forward_table(): return jnp.where(n[None, :] < ND, table, 0.0).astype(BF16)  26.7 us
    pallas_call x1, Pallas kernels, inverse(): call(inverse_kernel, jax.ShapeDtypeStruct((JD, 16, NLON), BF16), (3,), [p...  19.2 us
    pallas_call x1, Pallas kernels, mlp(): call(mlp_kernel, jax.ShapeDtypeStruct((NZ, 6, NP, 128), BF16), (6,), [pl....  17.6 us
  transfers between devices with their start and end apart: 5, of which 2 were waited for; matrix products, arithmetic and copies ran while one was open for 15% of the time, Pallas kernels for 16%

profile of v1, /device:TPU:1, one launch (start us, length us, event | category | flops | bytes accessed | tf_op | source)
XLA Modules:
  0.0 389.5 jit_solution(240548166139317456)
XLA Ops:
  6.5 17.6 %shard_map.56 = bf16[16,6,96,128]{3,2,1,0:T(8,128)(2,1)} custom-call(bf16[45,90,256]{2,1,0:T(8,128)(2,1)} %bitcast.5, f32[1,256]{1,0:T(1,128)} %bitcast.6, bf16[256,512]{1,0:T(8,128)(2,1)} %in_ref.1, bf16[512,256]{1,0:T(8,128)(2,1)} %out_w_ref.1), custom_call_target="tpu_custom_call" | custom-call | flops 2123366400 | bytes 5000000 | tf_op jit(solution)/shard_map/pallas_call | solution.py:93
  24.2 15.7 %all-to-all-start = ((bf16[16,6,96,128]{3,2,1,0:T(8,128)(2,1)}), bf16[16,6,96,128]{3,2,1,0:T(8,128)(2,1)S(1)}, u32[]{:S(2)}, u32[]{:S(2)}) async-start(bf16[16,6,96,128]{3,2,1,0:T(8,128)(2,1)} %shard_map.56), calls=%async_computation | async-start | bytes 4718592 | tf_op jit(solution)/shard_map/all_to_all | solution.py:524
  40.0 0.7 all-gather.3.cloned.1.call-update
  40.7 0.7 compare_select_fusion.weight_ref
  41.4 26.7 %fusion.4.table_ref = bf16[1024,1536]{1,0:T(8,128)(2,1)} fusion(s32[1024]{0:T(1024)S(1)} %get-tuple-element.10, s32[1536]{0:T(1024)S(1)} %fusion.21, s32[1024]{0:T(1024)S(1)} %get-tuple-element.9, pred[1536]{0:T(1024)(128)(4,1)S(1)} %fusion.25), kind=kLoop, calls=%fused_computation.6 | loop fusion | flops 18874368 | bytes 3161600 | tf_op jit(solution)/shard_map/convert_element_type | solution.py:480
  68.1 74.9 %all-to-all-done.x_ref = bf16[16,6,96,128]{3,2,1,0:T(8,128)(2,1)S(1)} async-done(((bf16[16,6,96,128]{3,2,1,0:T(8,128)(2,1)}), bf16[16,6,96,128]{3,2,1,0:T(8,128)(2,1)S(1)}, u32[]{:S(2)}, u32[]{:S(2)}) %all-to-all-start) | async-done | bytes 2359328 | tf_op jit(solution)/shard_map/all_to_all | solution.py:524
  143.0 1.4 copy-done
  144.4 17.3 %shard_map.57 = bf16[16,8,48,128]{3,2,1,0:T(8,128)(2,1)} custom-call(bf16[16,6,96,128]{3,2,1,0:T(8,128)(2,1)} %copy-done, bf16[1024,1536]{1,0:T(8,128)(2,1)} %fusion.4.table_ref, f32[3,1,256]{2,1,0:T(1,128)} %compare_select_fusion.weight_ref), custom_call_target="tpu_custom_call" | custom-call | flops 2415919104 | bytes 7000000 | tf_op jit(solution)/shard_map/pallas_call | solution.py:135
  161.7 11.6 %all-to-all-start.1 = ((bf16[16,8,48,128]{3,2,1,0:T(8,128)(2,1)}), bf16[16,8,48,128]{3,2,1,0:T(8,128)(2,1)S(1)}, u32[]{:S(2)}, u32[]{:S(2)}) async-start(bf16[16,8,48,128]{3,2,1,0:T(8,128)(2,1)} %shard_map.57), calls=%async_computation.1 | async-start | bytes 3145728 | tf_op jit(solution)/shard_map/all_to_all | solution.py:524
  173.8 0.7 add_select_fusion.2.log_ref
  174.5 0.7 broadcast_in_dim.81.order_ref
  175.7 31.0 %shard_map.55.table_ref = bf16[4,4,8,128,768]{4,3,2,1,0:T(8,128)(2,1)} custom-call(f32[4,8,128]{2,1,0:T(8,128)} %broadcast_in_dim.81.order_ref, f32[8,768]{1,0:T(8,128)} %broadcast_in_dim.83.cos_ref, f32[4,8,768]{2,1,0:T(8,128)} %add_select_fusion.2.log_ref), custom_call_target="tpu_custom_call" | custom-call | flops 200000000 | bytes 16000000 | tf_op jit(solution)/shard_map/pallas_call | solution.py:216
  206.8 1.1 copy-done.2
  207.9 14.5 %shard_map.58 = bf16[16,144,128]{2,1,0:T(8,128)(2,1)} custom-call(bf16[4,4,8,128,768]{4,3,2,1,0:T(8,128)(2,1)} %shard_map.55.table_ref, bf16[16,8,48,128]{3,2,1,0:T(8,128)(2,1)} %copy-done.2), custom_call_target="tpu_custom_call" | custom-call | flops 2013265920 | bytes 18000000 | tf_op jit(solution)/shard_map/pallas_call | solution.py:275
  222.4 7.0 %all-to-all-start.2 = ((bf16[16,144,128]{2,1,0:T(8,128)(2,1)}), bf16[16,144,128]{2,1,0:T(8,128)(2,1)S(1)}, u32[]{:S(2)}, u32[]{:S(2)}) async-start(bf16[16,144,128]{2,1,0:T(8,128)(2,1)} %shard_map.58), calls=%async_computation.2 | async-start | bytes 1179648 | tf_op jit(solution)/shard_map/all_to_all | solution.py:524
  229.5 26.1 %all-to-all-done.2.x_ref = bf16[16,144,128]{2,1,0:T(8,128)(2,1)S(1)} async-done(((bf16[16,144,128]{2,1,0:T(8,128)(2,1)}), bf16[16,144,128]{2,1,0:T(8,128)(2,1)S(1)}, u32[]{:S(2)}, u32[]{:S(2)}) %all-to-all-start.2) | async-done | bytes 589856 | tf_op jit(solution)/shard_map/all_to_all | solution.py:524
  255.5 0.8 copy-done.3
  256.4 8.2 %shard_map.59 = bf16[16,144,128]{2,1,0:T(8,128)(2,1)} custom-call(bf16[16,144,128]{2,1,0:T(8,128)(2,1)} %copy-done.3, bf16[16,2,256,256]{3,2,1,0:T(8,128)(2,1)} %bitcast.4), custom_call_target="tpu_custom_call" | custom-call | flops 150994944 | bytes 6000000 | tf_op jit(solution)/shard_map/pallas_call | solution.py:336
  264.6 45.6 %all_to_all.25.x_ref = bf16[16,144,128]{2,1,0:T(8,128)(2,1)} all-to-all(bf16[16,144,128]{2,1,0:T(8,128)(2,1)} %shard_map.59), channel_id=1, replica_groups=mesh['lat'=16,'lon'=16,'batch'=2] {'lon'}, dimensions={0} | all-to-all | bytes 1179648 | tf_op jit(solution)/shard_map/all_to_all | solution.py:524
  310.2 14.9 %shard_map.60 = bf16[16,8,48,128]{3,2,1,0:T(8,128)(2,1)} custom-call(bf16[4,4,8,128,768]{4,3,2,1,0:T(8,128)(2,1)} %shard_map.55.table_ref, bf16[16,144,128]{2,1,0:T(8,128)(2,1)} %all_to_all.25.x_ref), custom_call_target="tpu_custom_call" | custom-call | flops 503316480 | bytes 18000000 | tf_op jit(solution)/shard_map/pallas_call | solution.py:396
  325.2 9.4 %all-to-all-start.4 = ((bf16[16,8,48,128]{3,2,1,0:T(8,128)(2,1)}), bf16[16,8,48,128]{3,2,1,0:T(8,128)(2,1)S(1)}, u32[]{:S(2)}, u32[]{:S(2)}) async-start(bf16[16,8,48,128]{3,2,1,0:T(8,128)(2,1)} %shard_map.60), calls=%async_computation.4 | async-start | bytes 3145728 | tf_op jit(solution)/shard_map/all_to_all | solution.py:524
  334.6 27.6 %fusion.9.table_ref = bf16[1024,1440]{1,0:T(8,128)(2,1)} fusion(f32[1024]{0:T(1024)S(1)} %compare_select_fusion.4, s32[1024]{0:T(1024)S(1)} %get-tuple-element.10, s32[1024]{0:T(1024)S(1)} %get-tuple-element.9), kind=kLoop, calls=%fused_computation.11 | loop fusion | flops 17694720 | bytes 2961408 | tf_op jit(solution)/shard_map/convert_element_type | solution.py:487
  362.3 1.1 copy-done.1
  363.4 19.2 %shard_map.61 = bf16[45,16,1440]{2,1,0:T(8,128)(2,1)} custom-call(bf16[16,8,48,128]{3,2,1,0:T(8,128)(2,1)} %copy-done.1, bf16[16,6,96,128]{3,2,1,0:T(8,128)(2,1)} %copy-done, bf16[1024,1440]{1,0:T(8,128)(2,1)} %fusion.9.table_ref), custom_call_target="tpu_custom_call" | custom-call | flops 2264924160 | bytes 10000000 | tf_op jit(solution)/shard_map/pallas_call | solution.py:443
  (23 shorter events, 1.2 us)
Async XLA Ops:
  24.2 118.8 %all-to-all-start = ((bf16[16,6,96,128]{3,2,1,0:T(8,128)(2,1)}), bf16[16,6,96,128]{3,2,1,0:T(8,128)(2,1)S(1)}, u32[]{:S(2)}, u32[]{:S(2)}) async-start(bf16[16,6,96,128]{3,2,1,0:T(8,128)(2,1)} %shard_map.56), calls=%async_computation | async-start | bytes 4718592 | tf_op jit(solution)/shard_map/all_to_all | solution.py:524
  39.9 189.5 %all-gather.3.cloned.1.call-start = ((), (), s32[]{:S(2)}) async-start(), calls=%async_computation.5 | async-start | bytes 4456448 | tf_op jit(solution)/shard_map/all_gather | solution.py:531
  143.0 1.4 copy-start
  161.7 45.1 %all-to-all-start.1 = ((bf16[16,8,48,128]{3,2,1,0:T(8,128)(2,1)}), bf16[16,8,48,128]{3,2,1,0:T(8,128)(2,1)S(1)}, u32[]{:S(2)}, u32[]{:S(2)}) async-start(bf16[16,8,48,128]{3,2,1,0:T(8,128)(2,1)} %shard_map.57), calls=%async_computation.1 | async-start | bytes 3145728 | tf_op jit(solution)/shard_map/all_to_all | solution.py:524
  206.8 1.1 copy-start.2
  222.4 33.2 %all-to-all-start.2 = ((bf16[16,144,128]{2,1,0:T(8,128)(2,1)}), bf16[16,144,128]{2,1,0:T(8,128)(2,1)S(1)}, u32[]{:S(2)}, u32[]{:S(2)}) async-start(bf16[16,144,128]{2,1,0:T(8,128)(2,1)} %shard_map.58), calls=%async_computation.2 | async-start | bytes 1179648 | tf_op jit(solution)/shard_map/all_to_all | solution.py:524
  255.5 0.8 copy-start.3
  325.2 37.1 %all-to-all-start.4 = ((bf16[16,8,48,128]{3,2,1,0:T(8,128)(2,1)}), bf16[16,8,48,128]{3,2,1,0:T(8,128)(2,1)S(1)}, u32[]{:S(2)}, u32[]{:S(2)}) async-start(bf16[16,8,48,128]{3,2,1,0:T(8,128)(2,1)} %shard_map.60), calls=%async_computation.4 | async-start | bytes 3145728 | tf_op jit(solution)/shard_map/all_to_all | solution.py:524
  362.3 1.1 copy-start.1
Sparse Core Ops, SparseCore 0:
  44.1 73.4 all-gather.2

commit v2 on v1

v2 whole, which is shorter than its diff:
```python
import functools

import jax
import jax.numpy as jnp
from jax import lax
from jax.experimental import pallas as pl
from jax.experimental.pallas import tpu as pltpu
from jax.sharding import PartitionSpec as P

F32 = jnp.float32
BF16 = jnp.bfloat16

CH = 256
HID = 512
JD = 45
JP = 48
ND = 90
NP = 96
NLAT = 720
NLON = 1440
MODES = 512
NA = 16
NZ = 16
JH = NA * JP // 2
LAST = JD - 1
KB = 2 * MODES
ROWS = 144
LIMIT = 56 * 1024 * 1024
MESH = pl.DeviceIdType.MESH
OTHERS = (8, 7, 9, 6, 10, 5, 11, 4, 12, 3, 13, 2, 14, 1, 15)
PLACE = (0, 1, 7, 2, 3, 4, 5, 6)


def call(kernel, out_shape, grid, in_specs, out_specs, scratch, flops, moved):
    return pl.pallas_call(
        kernel,
        out_shape=out_shape,
        grid=grid,
        in_specs=in_specs,
        out_specs=out_specs,
        scratch_shapes=scratch,
        cost_estimate=pl.CostEstimate(flops=flops, bytes_accessed=moved, transcendentals=0),
        compiler_params=pltpu.CompilerParams(
            dimension_semantics=("arbitrary",) * len(grid), vmem_limit_bytes=LIMIT
        ),
    )


def swap_blocks(xs):
    block = lax.broadcasted_iota(jnp.int32, xs[0].shape, 1) // 16
    for bit in (1, 2, 4):
        upper = (block & bit) != 0
        new = list(xs)
        for i in range(8):
            if i & bit == 0:
                low, high = xs[i], xs[i | bit]
                new[i] = jnp.where(upper, pltpu.roll(high, 16 * bit, 1), low)
                new[i | bit] = jnp.where(upper, high, pltpu.roll(low, 128 - 16 * bit, 1))
        xs = new
    return xs


def greet(axes):
    barrier = pltpu.get_barrier_semaphore()
    for axis in axes:
        me = lax.axis_index(axis)
        for d in range(1, 16):
            pl.semaphore_signal(
                barrier, inc=1, device_id={axis: lax.rem(me + d, 16)}, device_id_type=MESH
            )
    pl.semaphore_wait(barrier, 15 * len(axes))


def to_peer(axis, d, src, dst, send, recv):
    peer = lax.rem(lax.axis_index(axis) + d, 16)
    return pltpu.make_async_remote_copy(
        src_ref=src(peer),
        dst_ref=dst,
        send_sem=send,
        recv_sem=recv,
        device_id={axis: peer},
        device_id_type=MESH,
    )


def band_row(jj):
    jj = jnp.minimum(jj, LAST)
    return jnp.where(lax.axis_index("lat") >= 8, LAST - jj, jj)


def mlp_chunk(g, x_ref, gain_ref, in_ref, out_w_ref, o_ref, pad_ref, mix_ref):
    for j in range(8):
        pad_ref[j * NP : j * NP + ND, :] = x_ref[band_row(8 * g + j)].astype(F32)
    half = 2 * NP
    for part in range(4):
        rows = slice(part * half, (part + 1) * half)
        x = pad_ref[rows, :]
        mean = jnp.mean(x, axis=1, keepdims=True)
        centered = x - mean
        spread = jnp.mean(centered * centered, axis=1, keepdims=True)
        normed = (centered * lax.rsqrt(spread + 1e-05) * gain_ref[...]).astype(BF16)
        hidden = jnp.dot(normed, in_ref[...], preferred_element_type=F32)
        hidden = jax.nn.gelu(hidden).astype(BF16)
        mixed = x + jnp.dot(hidden, out_w_ref[...], preferred_element_type=F32)
        mix_ref[0, rows, :] = mixed[:, :128]
        mix_ref[1, rows, :] = mixed[:, 128:]
    lane = lax.broadcasted_iota(jnp.int32, (16, 128), 1)
    row = lax.broadcasted_iota(jnp.int32, (16, 128), 0)
    live = lane // 16 < JD - 8 * g

    def place(step, _):
        start = pl.multiple_of(step * 16, 16)
        keep = jnp.logical_and(live, row < ND - start)
        for h in range(2):
            xs = [mix_ref[h, pl.ds(pl.multiple_of(j * NP + start, 16), 16), :] for j in range(8)]
            for z, y in enumerate(swap_blocks(xs)):
                o_ref[g, h * 8 + z, pl.ds(start, 16), :] = jnp.where(keep, y, 0.0).astype(BF16)
        return 0

    lax.fori_loop(0, NP // 16, place, 0)


def wave_table(basis_ref, o_ref, halve):
    width = o_ref.shape[1]
    group_cos, group_sin = basis_ref[4, :, :width], basis_ref[5, :, :width]
    row = lax.broadcasted_iota(jnp.int32, (8, width), 0)

    def step(high, _):
        high_cos = basis_ref[2, pl.ds(high, 1), :width]
        high_sin = basis_ref[3, pl.ds(high, 1), :width]
        for low in range(8):
            low_cos = basis_ref[0, low : low + 1, :width]
            low_sin = basis_ref[1, low : low + 1, :width]
            c = high_cos * low_cos - high_sin * low_sin
            s = high_sin * low_cos + high_cos * low_sin
            real = group_cos * c - group_sin * s
            imag = -(group_sin * c + group_cos * s)
            if halve and low == 0:
                real = jnp.where(jnp.logical_and(high == 0, row == 0), 0.5 * real, real)
            offset = 8 * high + low
            start = offset // 2 % 16 * 64 + offset // 32 * 32 + low % 2 * 16
            o_ref[pl.ds(pl.multiple_of(start, 16), 16), :] = jnp.concatenate(
                [real, imag], axis=0
            ).astype(BF16)
        return 0

    lax.fori_loop(0, 8, step, 0)


def wave_basis(points, scale, order):
    count = jnp.arange(8, dtype=jnp.int32)
    multiple = jnp.stack([count, 8 * count, 64 * jnp.array(order, jnp.int32)])
    phase = multiple[:, :, None] * points[None, None, :] % NLON
    angle = 2.0 * jnp.pi / NLON * phase.astype(F32)
    factor = jnp.stack([jnp.ones_like(scale), jnp.ones_like(scale), scale])[:, None, :]
    return jnp.stack([jnp.cos(angle) * factor, jnp.sin(angle) * factor], axis=1).reshape(
        6, 8, points.shape[0]
    )


def forward_basis():
    column = jnp.arange(NZ * NP, dtype=jnp.int32)
    n = column % NP
    return wave_basis(column // NP * ND + n, jnp.where(n < ND, 1.0, 0.0), tuple(range(8)))


def inverse_basis():
    return wave_basis(jnp.arange(NLON, dtype=jnp.int32), jnp.full((NLON,), 2.0, F32), PLACE)


def dft_pair(x_ref, gp, table_ref, weight_ref, o_ref, acc_ref, swap_ref):
    both = jnp.concatenate(
        [x_ref[2 * gp + gg].reshape(NZ * NP, 128) for gg in range(2)], axis=1
    )
    for part in range(4):
        rows = slice(part * 256, (part + 1) * 256)
        acc = jnp.dot(table_ref[rows, :], both, preferred_element_type=F32)
        acc = acc * weight_ref[gp]
        acc_ref[0, rows, :] = acc[:, :128]
        acc_ref[1, rows, :] = acc[:, 128:]

    def place(a, _):
        for gg in range(2):
            xs = [
                acc_ref[gg, pl.ds(pl.multiple_of(a * 64 + mr * 8, 8), 8), :] for mr in range(8)
            ]
            for j, y in enumerate(swap_blocks(xs)):
                swap_ref[pl.ds(gg * 8 + j, 8, stride=16), :] = y
        o_ref[gp, a] = swap_ref[...].astype(BF16).reshape(8, 16, 128)
        return 0

    lax.fori_loop(0, NA, place, 0)


def legendre_group(q, i, order_ref, cos_ref, o_ref, up_ref, low_ref, scale_ref, swap_ref):
    order = order_ref[q]
    degree = lax.broadcasted_iota(jnp.int32, (8, 128), 1) + 16 * i
    degree = degree.astype(F32)
    active = degree > order
    second = degree > order + 1.0
    grow = jnp.sqrt(
        jnp.where(active, 4.0 * degree * degree - 1.0, 0.0)
        / jnp.where(active, degree * degree - order * order, 1.0)
    )
    before = degree - 1.0
    damp = grow * jnp.sqrt(
        jnp.where(second, before * before - order * order, 0.0)
        / jnp.where(second, 4.0 * before * before - 1.0, 1.0)
    )
    first = jnp.where(degree == order, 1.0, 0.0)
    up, low, scale_log = up_ref[q], low_ref[q], scale_ref[q]
    root = jnp.exp(0.5 * scale_log)
    cosine = cos_ref[...]
    for s in range(16):
        a = jnp.broadcast_to(grow[:, s : s + 1], (8, JH))
        b = jnp.broadcast_to(damp[:, s : s + 1], (8, JH))
        e = jnp.broadcast_to(first[:, s : s + 1], (8, JH))
        fresh = a * (cosine * up) - b * low + e
        low = up
        up = fresh
        value = fresh * root * root
        for k in range(3):
            swap_ref[q, k, s * 8 : s * 8 + 8, :] = value[:, k * 128 : k * 128 + 128]
    largest = jnp.maximum(jnp.abs(up), jnp.abs(low))
    largest = jnp.where(largest > 0.0, largest, 1.0)
    up_ref[q] = up / largest
    low_ref[q] = low / largest
    scale_ref[q] = scale_log + jnp.log(largest)
    start = pl.multiple_of(i * 16, 16)
    for m in range(8):
        for k in range(3):
            o_ref[8 * q + m, pl.ds(start, 16), k * 128 : k * 128 + 128] = swap_ref[
                q, k, pl.ds(m, 16, stride=8), :
            ].astype(BF16)


def legendre(order_ref, cos_ref, log_ref, o_ref, up_ref, low_ref, scale_ref, swap_ref):
    up_ref[...] = jnp.zeros_like(up_ref)
    low_ref[...] = jnp.zeros_like(low_ref)
    scale_ref[...] = log_ref[...]
    for stage in range(4):

        def step(i, _, stage=stage):
            for q in range(stage + 1):
                legendre_group(
                    q, i, order_ref, cos_ref, o_ref, up_ref, low_ref, scale_ref, swap_ref
                )
            return 0

        lax.fori_loop(8 * stage, 8 * stage + 8, step, 0)


def forward_kernel(
    x_ref,
    gain_ref,
    in_ref,
    out_w_ref,
    basis_ref,
    weight_ref,
    order_ref,
    cos_ref,
    log_ref,
    rows_ref,
    spectrum_ref,
    legendre_ref,
    pad_ref,
    mix_ref,
    out_rows,
    got_rows,
    table_ref,
    acc_ref,
    swap_ref,
    out_spectrum,
    table_l,
    up_ref,
    low_ref,
    scale_ref,
    swap_l,
    z_send,
    z_recv,
    a_send,
    a_recv,
    own,
):
    lat = lax.axis_index("lat")
    lon = lax.axis_index("lon")

    def row_copy(g, d):
        return to_peer(
            "lon",
            d,
            lambda peer: out_rows.at[g, peer],
            got_rows.at[g, lon],
            z_send.at[g, d],
            z_recv.at[g, d],
        )

    def spectrum_copy(gp, d):
        return to_peer(
            "lat",
            d,
            lambda peer: out_spectrum.at[gp, peer],
            spectrum_ref.at[gp, lat],
            a_send.at[gp, d],
            a_recv.at[gp, d],
        )

    def own_row(g):
        return pltpu.make_async_copy(out_rows.at[g, lon], got_rows.at[g, lon], own.at[0, g])

    def own_spectrum(gp):
        return pltpu.make_async_copy(
            out_spectrum.at[gp, lat], spectrum_ref.at[gp, lat], own.at[1, gp]
        )

    def keep_rows(gp):
        pair = pl.ds(2 * gp, 2)
        return pltpu.make_async_copy(got_rows.at[pair], rows_ref.at[pair], own.at[2, gp])

    def keep_table(q):
        part = (pl.ds(8 * q, 8), pl.ds(128 * q, MODES - 128 * q))
        return pltpu.make_async_copy(table_l.at[part], legendre_ref.at[part], own.at[3, q])

    greet(("lat", "lon"))

    def mlp_step(g, _):
        mlp_chunk(g, x_ref, gain_ref, in_ref, out_w_ref, out_rows, pad_ref, mix_ref)
        for d in OTHERS:
            row_copy(g, d).start()
        own_row(g).start()
        return 0

    pad_ref[...] = jnp.zeros_like(pad_ref)
    lax.fori_loop(0, 6, mlp_step, 0)
    wave_table(basis_ref, table_ref, False)
    legendre(order_ref, cos_ref, log_ref, table_l, up_ref, low_ref, scale_ref, swap_l)
    for q in range(4):
        keep_table(q).start()

    def dft_step(gp, _):
        for gg in range(2):
            own_row(2 * gp + gg).wait()
            for d in OTHERS:
                row_copy(2 * gp + gg, d).wait_recv()
        keep_rows(gp).start()
        dft_pair(got_rows, gp, table_ref, weight_ref, out_spectrum, acc_ref, swap_ref)
        for d in OTHERS:
            spectrum_copy(gp, d).start()
        own_spectrum(gp).start()
        return 0

    lax.fori_loop(0, 3, dft_step, 0)
    for q in range(4):
        keep_table(q).wait()

    def finish(gp, _):
        for gg in range(2):
            for d in OTHERS:
                row_copy(2 * gp + gg, d).wait_send()
        keep_rows(gp).wait()
        own_spectrum(gp).wait()
        for d in OTHERS:
            spectrum_copy(gp, d).wait()
        return 0

    lax.fori_loop(0, 3, finish, 0)


VM = pl.BlockSpec(memory_space=pltpu.VMEM)
ANY = pl.BlockSpec(memory_space=pl.ANY)


def forward(*operands):
    return pl.pallas_call(
        forward_kernel,
        out_shape=(
            jax.ShapeDtypeStruct((6, NZ, NP, 128), BF16),
            jax.ShapeDtypeStruct((3, NA, 8, 16, 128), BF16),
            jax.ShapeDtypeStruct((32, MODES, JH), BF16),
        ),
        in_specs=[VM] * len(operands),
        out_specs=(ANY, ANY, ANY),
        scratch_shapes=[
            pltpu.VMEM((8 * NP, CH), F32),
            pltpu.VMEM((2, 8 * NP, 128), F32),
            pltpu.VMEM((6, NZ, NP, 128), BF16),
            pltpu.VMEM((6, NZ, NP, 128), BF16),
            pltpu.VMEM((KB, NZ * NP), BF16),
            pltpu.VMEM((2, KB, 128), F32),
            pltpu.VMEM((128, 128), F32),
            pltpu.VMEM((3, NA, 8, 16, 128), BF16),
            pltpu.VMEM((32, MODES, JH), BF16),
            pltpu.VMEM((4, 8, JH), F32),
            pltpu.VMEM((4, 8, JH), F32),
            pltpu.VMEM((4, 8, JH), F32),
            pltpu.VMEM((4, 3, 128, 128), F32),
            pltpu.SemaphoreType.DMA((6, 16)),
            pltpu.SemaphoreType.DMA((6, 16)),
            pltpu.SemaphoreType.DMA((3, 16)),
            pltpu.SemaphoreType.DMA((3, 16)),
            pltpu.SemaphoreType.DMA((4, 6)),
        ],
        cost_estimate=pl.CostEstimate(
            flops=8_000_000_000, bytes_accessed=30_000_000, transcendentals=0
        ),
        compiler_params=pltpu.CompilerParams(
            collective_id=1, has_side_effects=True, vmem_limit_bytes=LIMIT
        ),
    )(*operands)


def analyse(mg, x_ref, table, all_ref):
    north, south = [], []
    for gp in range(3):
        north.append(x_ref[gp, :8, mg].reshape(128, 128).astype(F32))
        south.append(jnp.concatenate([x_ref[gp, 15 - a, mg] for a in range(8)], axis=0).astype(F32))
    north = jnp.concatenate(north, axis=0)
    south = jnp.concatenate(south, axis=0)
    both = jnp.concatenate([north + south, north - south], axis=1).astype(BF16)
    block = lax.broadcasted_iota(jnp.int32, (128, 128), 1) // 32
    odd = lax.broadcasted_iota(jnp.int32, (128, 128), 0) % 2 == 1
    for lb in range(mg // 2, 4):
        rows = slice(lb * 128, lb * 128 + 128)
        total = jnp.zeros((128, 128), F32)
        for m in range(4):
            part = jnp.dot(table(m, rows), both, preferred_element_type=F32)
            first, second = part[:, :128], part[:, 128:]
            if m % 2:
                first, second = second, first
            total = jnp.where(block == m, jnp.where(odd, second, first), total)
        all_ref[mg, rows, :] = total


def analysis_rows(z, all_ref, o_ref):
    row = lax.broadcasted_iota(jnp.int32, (16, 128), 0)
    kept = []
    for t in range(2):
        parts = [all_ref[g, pl.ds(2 * z + t, 16, stride=32), :] for g in range(8)]
        o_ref[z, t * 16 : t * 16 + 16, :] = parts[0].astype(BF16)
        for s in range(1, 4):
            both = jnp.where(row < 2 * s, pltpu.roll(parts[8 - s], 2 * s, 0), parts[s])
            o_ref[z, s * 32 + t * 16 : s * 32 + t * 16 + 16, :] = both.astype(BF16)
        kept.append(parts[4][8:])
    o_ref[z, 128:144, :] = jnp.concatenate(kept, axis=0).astype(BF16)


def analysis_kernel(table_ref, x_ref, o_ref, all_ref):
    q = pl.program_id(0)
    for mg in range(8):

        @pl.when(q == mg // 2)
        def _(mg=mg):
            analyse(mg, x_ref, lambda m, rows: table_ref[mg % 2 * 4 + m, rows, :], all_ref)

    @pl.when(q == 3)
    def _():
        def place(z, _):
            analysis_rows(z, all_ref, o_ref)
            return 0

        lax.fori_loop(0, NZ, place, 0)


def analysis(table, fields):
    return call(
        analysis_kernel,
        jax.ShapeDtypeStruct((NZ, ROWS, 128), BF16),
        (4,),
        [
            pl.BlockSpec((8, MODES, JH), lambda q: (q, 0, 0)),
            pl.BlockSpec((3, NA, 8, 16, 128), lambda q: (0, 0, 0, 0, 0)),
        ],
        pl.BlockSpec((NZ, ROWS, 128), lambda q: (0, 0, 0)),
        [pltpu.VMEM((8, MODES, 128), F32)],
        2 * 80 * 128 * JH * 256,
        18_000_000,
    )(table, fields)


def filter_row(mg, a, t):
    if mg < 4:
        return 32 * mg + 16 * t + a
    if mg == 4:
        return 128 + 8 * t + a - 8
    return 32 * (8 - mg) + 16 * t + a - 2 * mg


def filter_kernel(x_ref, w_ref, o_ref, in_ref, out_ref):
    def gather(step, _):
        start = pl.multiple_of(step * 16, 16)
        for h in range(2):
            xs = [x_ref[h * 8 + z, pl.ds(start, 16), :].astype(F32) for z in range(8)]
            for mr, y in enumerate(swap_blocks(xs)):
                in_ref[h, pl.ds(start * 8 + mr, 16, stride=8), :] = y
        return 0

    lax.fori_loop(0, ROWS // 16, gather, 0)
    for a in range(16):
        for t in range(2):
            rows = [8 * filter_row(mg, a, t) for mg in range(a // 2 + 1)]
            x = jnp.concatenate(
                [
                    jnp.concatenate([in_ref[h, r : r + 8, :] for r in rows], axis=0)
                    for h in range(2)
                ],
                axis=1,
            ).astype(BF16)
            y = jnp.dot(x, w_ref[a, t], preferred_element_type=F32)
            for i, r in enumerate(rows):
                for h in range(2):
                    out_ref[h, r : r + 8, :] = y[i * 8 : i * 8 + 8, h * 128 : h * 128 + 128]

    def scatter(step, _):
        start = pl.multiple_of(step * 16, 16)
        for h in range(2):
            xs = [out_ref[h, pl.ds(start * 8 + mr, 16, stride=8), :] for mr in range(8)]
            for z, y in enumerate(swap_blocks(xs)):
                o_ref[h * 8 + z, pl.ds(start, 16), :] = y.astype(BF16)
        return 0

    lax.fori_loop(0, ROWS // 16, scatter, 0)


def channel_filter(coefficients, weight):
    whole = pl.BlockSpec((NZ, ROWS, 128), lambda i: (0, 0, 0))
    return call(
        filter_kernel,
        jax.ShapeDtypeStruct((NZ, ROWS, 128), BF16),
        (1,),
        [whole, pl.BlockSpec((NA, 2, CH, CH), lambda i: (0, 0, 0, 0))],
        whole,
        [pltpu.VMEM((2, ROWS * 8, 128), F32), pltpu.VMEM((2, ROWS * 8, 128), F32)],
        2 * ROWS * 8 * CH * CH,
        6_000_000,
    )(coefficients, weight)


def synthesis_rows(z, x_ref, all_ref):
    row = lax.broadcasted_iota(jnp.int32, (16, 128), 0)
    last = x_ref[z, 128:144, :].astype(F32)
    for t in range(2):
        where = pl.ds(2 * z + t, 16, stride=32)
        all_ref[0, where, :] = x_ref[z, t * 16 : t * 16 + 16, :].astype(F32)
        for s in range(1, 4):
            x = x_ref[z, s * 32 + t * 16 : s * 32 + t * 16 + 16, :].astype(F32)
            all_ref[s, where, :] = jnp.where(row >= 2 * s, x, 0.0)
            all_ref[8 - s, where, :] = jnp.where(
                row >= 16 - 2 * s, pltpu.roll(x, 16 - 2 * s, 0), 0.0
            )
        all_ref[4, where, :] = jnp.concatenate(
            [jnp.zeros((8, 128), F32), last[t * 8 : t * 8 + 8]], axis=0
        )


def synthesise(mg, table, all_ref, o_ref):
    low = mg // 2 * 128
    block = lax.broadcasted_iota(jnp.int32, (MODES - low, 128), 1) // 32
    row = lax.broadcasted_iota(jnp.int32, (MODES - low, 128), 0)
    same = (block + row) % 2 == 0
    x = all_ref[mg, low:, :]
    even = jnp.where(same, x, 0.0).T.astype(BF16)
    odd = jnp.where(same, 0.0, x).T.astype(BF16)
    evens, odds = [], []
    for m in range(4):
        rows = slice(m * 32, m * 32 + 32)
        both = jnp.concatenate([even[rows], odd[rows]], axis=0)
        part = jnp.dot(both, table(m, slice(low, MODES)), preferred_element_type=F32)
        evens.append(part[:32])
        odds.append(part[32:])
    even = jnp.concatenate(evens, axis=0).T
    odd = jnp.concatenate(odds, axis=0).T
    north = (even + odd).astype(BF16)
    south = (even - odd).astype(BF16)
    place = PLACE.index(mg)
    for gp in range(3):
        for a in range(8):
            rows = slice(gp * 128 + a * 16, gp * 128 + a * 16 + 16)
            o_ref[a, place, gp] = north[rows]
            o_ref[15 - a, place, gp] = south[rows]


def synthesis_kernel(table_ref, x_ref, o_ref, all_ref):
    q = pl.program_id(0)

    @pl.when(q == 0)
    def _():
        def place(z, _):
            synthesis_rows(z, x_ref, all_ref)
            return 0

        lax.fori_loop(0, NZ, place, 0)

    for mg in range(8):

        @pl.when(q == mg // 2)
        def _(mg=mg):
            synthesise(mg, lambda m, rows: table_ref[mg % 2 * 4 + m, rows, :], all_ref, o_ref)


def synthesis(table, filtered):
    return call(
        synthesis_kernel,
        jax.ShapeDtypeStruct((NA, 8, 3, 16, 128), BF16),
        (4,),
        [
            pl.BlockSpec((8, MODES, JH), lambda q: (q, 0, 0)),
            pl.BlockSpec((NZ, ROWS, 128), lambda q: (0, 0, 0)),
        ],
        pl.BlockSpec((NA, 8, 3, 16, 128), lambda q: (0, 0, 0, 0, 0)),
        [pltpu.VMEM((8, MODES, 128), F32)],
        2 * 80 * 128 * JH * 64,
        18_000_000,
    )(table, filtered)


def inverse_pair(gp, u_ref, x_ref, table_ref, o_ref, wide_ref, rows_ref, lhs_ref, acc_ref):
    def place(a, _):
        wide_ref[...] = u_ref[a, :, gp].reshape(128, 128).astype(F32)
        for gg in range(2):
            xs = [wide_ref[pl.ds(gg * 8 + j, 8, stride=16), :] for j in range(8)]
            for mr, y in enumerate(swap_blocks(xs)):
                rows_ref[gg, pl.ds(pl.multiple_of(a * 64 + mr * 8, 8), 8), :] = y
        return 0

    lax.fori_loop(0, NA, place, 0)
    for gg in range(2):
        for k in range(8):
            cols = slice(k * 128, (k + 1) * 128)
            lhs_ref[gg * 128 : gg * 128 + 128, cols] = rows_ref[gg, cols, :].T.astype(BF16)
    for part in range(2):
        rows = slice(part * 128, part * 128 + 128)
        acc_ref[rows, :NLON] = jnp.dot(lhs_ref[rows, :], table_ref[...], preferred_element_type=F32)
    row = lax.broadcasted_iota(jnp.int32, (NP, 256), 0)
    lane = lax.broadcasted_iota(jnp.int32, (NP, 256), 1)
    for z in range(NZ):
        begin = ND * z // 128 * 128
        pick = jnp.logical_and(lane == row + (ND * z - begin), row < ND)
        pick = jnp.where(pick, 1.0, 0.0).astype(BF16)
        x = jnp.concatenate([x_ref[2 * gp + gg, z].astype(F32).T for gg in range(2)], axis=0)
        acc_ref[:, begin : begin + 256] += jnp.dot(
            x.astype(BF16), pick, preferred_element_type=F32
        )
    for j in range(16):

        @pl.when(16 * gp + j < JD)
        def _(j=j):
            o_ref[band_row(16 * gp + j)] = acc_ref[16 * j : 16 * j + 16, :NLON].astype(BF16)


def inverse_kernel(
    u_ref, x_ref, basis_ref, o_ref, table_ref, wide_ref, rows_ref, lhs_ref, acc_ref
):
    gp = pl.program_id(0)

    @pl.when(gp == 0)
    def _():
        wave_table(basis_ref, table_ref, True)

    inverse_pair(gp, u_ref, x_ref, table_ref, o_ref, wide_ref, rows_ref, lhs_ref, acc_ref)


def inverse(waves, fields, basis):
    return call(
        inverse_kernel,
        jax.ShapeDtypeStruct((JD, 16, NLON), BF16),
        (3,),
        [
            pl.BlockSpec((NA, 8, 3, 16, 128), lambda g: (0, 0, 0, 0, 0)),
            pl.BlockSpec((6, NZ, NP, 128), lambda g: (0, 0, 0, 0)),
            pl.BlockSpec((6, 8, NLON), lambda g: (0, 0, 0)),
        ],
        pl.BlockSpec((JD, 16, NLON), lambda g: (0, 0, 0)),
        [
            pltpu.VMEM((KB, NLON), BF16),
            pltpu.VMEM((128, 128), F32),
            pltpu.VMEM((2, KB, 128), F32),
            pltpu.VMEM((256, KB), BF16),
            pltpu.VMEM((256, 1536), F32),
        ],
        2 * KB * NLON * 768,
        10_000_000,
    )(waves, fields, basis)


def legendre_inputs(lat_index):
    slot = jnp.arange(32, dtype=jnp.int32)
    orders = (32 * (slot // 2) + 2 * lat_index + slot % 2).astype(F32)
    column = jnp.arange(JH, dtype=jnp.int32)
    local = column // 128 * 16 + column % 16
    theta = jnp.pi * ((column // 16 % 8 * JD + local).astype(F32) + 0.5) / NLAT
    real = local < JD
    cosine = jnp.where(real, jnp.cos(theta), 0.0)
    log_sine = jnp.log(jnp.where(real, jnp.sin(theta), 1.0))
    counts = jnp.arange(1, MODES + 1, dtype=F32)
    ratios = jnp.log((2.0 * counts - 1.0) / (2.0 * counts))
    partial_log = jnp.sum(jnp.where(counts[None, :] <= orders[:, None], ratios[None, :], 0.0), axis=1)
    start_log = (
        orders[:, None] * log_sine[None, :]
        + 0.5 * jnp.log(orders + 0.5)[:, None]
        + 0.5 * partial_log[:, None]
    )
    start_log = jnp.where(real[None, :], start_log, -1e9)
    return (
        jnp.broadcast_to(orders.reshape(4, 8, 1), (4, 8, 128)),
        jnp.broadcast_to(cosine[None, :], (8, JH)),
        start_log.reshape(4, 8, JH),
    )


def spectrum_weights(lat_index):
    local = jnp.arange(6 * 128, dtype=jnp.int32) // 16
    band = jnp.minimum(lat_index, 15 - lat_index)
    theta = jnp.pi * ((band * JD + local).astype(F32) + 0.5) / NLAT
    weights = jnp.pi / NLAT * jnp.sin(theta) / NLON
    return jnp.where(local < JD, weights, 0.0).reshape(3, 1, 256)


def exchange(x, axis):
    return lax.all_to_all(x, axis, split_axis=0, concat_axis=0, tiled=True)


def on_device(grid, norm_gain, mlp_in, mlp_out, filter_weight):
    lat_index = lax.axis_index("lat")
    weight = lax.all_gather(filter_weight, "lat")
    rows, spectrum, table = forward(
        grid.transpose(1, 2, 0),
        norm_gain.reshape(1, CH),
        mlp_in,
        mlp_out,
        forward_basis(),
        spectrum_weights(lat_index),
        *legendre_inputs(lat_index),
    )
    coefficients = analysis(table, spectrum)
    filtered = channel_filter(exchange(coefficients, "lon"), weight)
    synthesized = synthesis(table, exchange(filtered, "lon"))
    updated = inverse(exchange(synthesized, "lat"), rows, inverse_basis())
    return updated.transpose(1, 0, 2)


def solution(mesh):
    return jax.shard_map(
        on_device,
        mesh=mesh,
        in_specs=(P("batch", "lat", "lon"), P(), P(), P(), P(("lat", "lon"), None, None)),
        out_specs=P(("batch", "lon"), "lat", None),
        check_vma=False,
    )
```

time: 390 us -> 318 us (0.82)
  waiting for transfers between devices: 102 us -> 22.2 us
  Pallas kernels: 123 us -> 190 us
  other arithmetic: 56.2 us -> 5.36 us
  starting transfers between devices: 43.8 us -> 7.33 us
  blocking collectives: 45.6 us -> 76.4 us
    all_to_all x4 -> x1, waiting for transfers between devices: 101 us -> 21.5 us  [exchange(): return lax.all_to_all(x, axis, split_axis=0, concat_axis=0, tiled=True)]
    pallas_call x5 -> x3, Pallas kernels: 95.4 us -> 160 us  [the longest x1 141 us: forward(): pl.pallas_call(forward_kernel, out_shape=(jax.ShapeDtypeStruct((6, NZ, NP...]
    convert_element_type x2 -> x0, other arithmetic: 54.3 us -> none  [the longest x1 27.6 us: inverse_table(): return (table * amplitude[:, None]).astype(BF16)]
    all_to_all x4 -> x1, starting transfers between devices: 43.7 us -> 7.33 us  [exchange(): return lax.all_to_all(x, axis, split_axis=0, concat_axis=0, tiled=True)]
    all_to_all x1 -> x2, blocking collectives: 45.6 us -> 76.4 us  [exchange(): return lax.all_to_all(x, axis, split_axis=0, concat_axis=0, tiled=True)]
  transfers between devices with their start and end apart: 5 -> 2, of which waited for: 2 -> 1; matrix products, arithmetic and copies ran while one was open for 15% -> 2% of each run, Pallas kernels for 16% -> 47%
where the time goes in v2:
time: 318 us
  Pallas kernels  190 us (60%)
  blocking collectives  76.4 us (24%)
  waiting for transfers between devices  22.2 us (7%)
  between operations  13.5 us (4%)
  starting transfers between devices  7.33 us (2%)
  other arithmetic  5.36 us (2%)
    pallas_call x1, Pallas kernels, forward(): pl.pallas_call(forward_kernel, out_shape=(jax.ShapeDtypeStruct((6, NZ, NP...  141 us
    all_to_all x2, blocking collectives, exchange(): return lax.all_to_all(x, axis, split_axis=0, concat_axis=0, tiled=True)  76.4 us
    pallas_call x1, Pallas kernels, inverse(): call(inverse_kernel, jax.ShapeDtypeStruct((JD, 16, NLON), BF16), (3,), [p...  21.9 us
    all_to_all x1, waiting for transfers between devices, exchange(): return lax.all_to_all(x, axis, split_axis=0, concat_axis=0, tiled=True)  21.5 us
    pallas_call x1, Pallas kernels, analysis(): call(analysis_kernel, jax.ShapeDtypeStruct((NZ, ROWS, 128), BF16), (4,),...  9.81 us
    pallas_call x1, Pallas kernels, synthesis(): call(synthesis_kernel, jax.ShapeDtypeStruct((NA, 8, 3, 16, 128), BF16), (...  9.76 us
    pallas_call x1, Pallas kernels, channel_filter(): call(filter_kernel, jax.ShapeDtypeStruct((NZ, ROWS, 128), BF16), (1,), [w...  8.22 us
    all_to_all x1, starting transfers between devices, exchange(): return lax.all_to_all(x, axis, split_axis=0, concat_axis=0, tiled=True)  7.33 us
  transfers between devices with their start and end apart: 2, of which 1 were waited for; matrix products, arithmetic and copies ran while one was open for 2% of the time, Pallas kernels for 47%

profile of v2, /device:TPU:1, one launch (start us, length us, event | category | flops | bytes accessed | tf_op | source)
XLA Modules:
  0.0 317.8 jit_solution(12947866914498176154)
XLA Ops:
  6.5 0.0 all-gather.3.cloned.1.call-start
  6.5 0.7 all-gather.3.cloned.1.call-update
  7.3 0.2 select_reduce_fusion
  7.5 0.1 mul.304
  7.7 0.1 select_log_fusion
  7.8 0.7 compare_select_fusion.1.weight_ref
  8.5 0.7 pad_add_fusion.2
  9.2 0.7 add_select_fusion.2.log_ref
  9.9 0.7 cosine_multiply_fusion.1
  10.6 0.7 pad_maximum_fusion
  11.4 0.7 broadcast_in_dim.70.order_ref
  12.0 0.6 broadcast_in_dim.72.cos_ref
  12.6 140.8 %shard_map.73 = (bf16[6,16,96,128]{3,2,1,0:T(8,128)(2,1)}, bf16[3,16,8,16,128]{4,3,2,1,0:T(8,128)(2,1)}, bf16[32,512,384]{2,1,0:T(8,128)(2,1)}) custom-call(bf16[45,90,256]{2,1,0:T(8,128)(2,1)} %bitcast.11, f32[1,256]{1,0:T(1,128)} %bitcast.12, bf16[256,512]{1,0:T(8,128)(2,1)} %in_ref.1, bf16[512,256]{1,0:T(8,128)(2,1)} %out_w_ref.1, f32[6,8,1536]{2,1,0:T(8,128)} %bitcast.9, ...), custom_call_target="tpu_custom_call" | custom-call | flops 8000000000 | bytes 30000000 | tf_op jit(solution)/shard_map/pallas_call | solution.py:374
  153.4 9.8 %shard_map.74 = bf16[16,144,128]{2,1,0:T(8,128)(2,1)} custom-call(bf16[32,512,384]{2,1,0:T(8,128)(2,1)} %get-tuple-element.8.table_ref, bf16[3,16,8,16,128]{4,3,2,1,0:T(8,128)(2,1)} %get-tuple-element.9.x_ref), custom_call_target="tpu_custom_call" | custom-call | flops 2013265920 | bytes 18000000 | tf_op jit(solution)/shard_map/pallas_call | solution.py:465
  163.2 37.6 %all_to_all.15.x_ref = bf16[16,144,128]{2,1,0:T(8,128)(2,1)} all-to-all(bf16[16,144,128]{2,1,0:T(8,128)(2,1)} %shard_map.74), channel_id=1, replica_groups=mesh['lat'=16,'lon'=16,'batch'=2] {'lon'}, dimensions={0} | all-to-all | bytes 1179648 | tf_op jit(solution)/shard_map/all_to_all | solution.py:719
  200.8 8.2 %shard_map.75 = bf16[16,144,128]{2,1,0:T(8,128)(2,1)} custom-call(bf16[16,144,128]{2,1,0:T(8,128)(2,1)} %all_to_all.15.x_ref, bf16[16,2,256,256]{3,2,1,0:T(8,128)(2,1)} %bitcast.8), custom_call_target="tpu_custom_call" | custom-call | flops 150994944 | bytes 6000000 | tf_op jit(solution)/shard_map/pallas_call | solution.py:526
  209.0 38.8 %all_to_all.16.x_ref = bf16[16,144,128]{2,1,0:T(8,128)(2,1)} all-to-all(bf16[16,144,128]{2,1,0:T(8,128)(2,1)} %shard_map.75), channel_id=1, replica_groups=mesh['lat'=16,'lon'=16,'batch'=2] {'lon'}, dimensions={0} | all-to-all | bytes 1179648 | tf_op jit(solution)/shard_map/all_to_all | solution.py:719
  247.8 9.8 %shard_map.76 = bf16[16,8,3,16,128]{4,3,2,1,0:T(8,128)(2,1)} custom-call(bf16[32,512,384]{2,1,0:T(8,128)(2,1)} %get-tuple-element.8.table_ref, bf16[16,144,128]{2,1,0:T(8,128)(2,1)} %all_to_all.16.x_ref), custom_call_target="tpu_custom_call" | custom-call | flops 503316480 | bytes 18000000 | tf_op jit(solution)/shard_map/pallas_call | solution.py:601
  257.6 7.3 %all-to-all-start.2 = ((bf16[16,8,3,16,128]{4,3,2,1,0:T(8,128)(2,1)}), bf16[16,8,3,16,128]{4,3,2,1,0:T(8,128)(2,1)S(1)}, u32[]{:S(2)}, u32[]{:S(2)}) async-start(bf16[16,8,3,16,128]{4,3,2,1,0:T(8,128)(2,1)} %shard_map.76), calls=%async_computation.2 | async-start | bytes 3145728 | tf_op jit(solution)/shard_map/all_to_all | solution.py:719
  264.9 0.7 cosine_multiply_fusion
  265.6 0.7 pad_maximum_fusion.1
  266.4 21.5 %all-to-all-done.2.u_ref = bf16[16,8,3,16,128]{4,3,2,1,0:T(8,128)(2,1)S(1)} async-done(((bf16[16,8,3,16,128]{4,3,2,1,0:T(8,128)(2,1)}), bf16[16,8,3,16,128]{4,3,2,1,0:T(8,128)(2,1)S(1)}, u32[]{:S(2)}, u32[]{:S(2)}) %all-to-all-start.2) | async-done | bytes 1572896 | tf_op jit(solution)/shard_map/all_to_all | solution.py:719
  287.9 1.1 copy-done
  289.1 21.9 %shard_map.77 = bf16[45,16,1440]{2,1,0:T(8,128)(2,1)} custom-call(bf16[16,8,3,16,128]{4,3,2,1,0:T(8,128)(2,1)} %copy-done, bf16[6,16,96,128]{3,2,1,0:T(8,128)(2,1)} %get-tuple-element.10.x_ref, f32[6,8,1440]{2,1,0:T(8,128)} %bitcast.10), custom_call_target="tpu_custom_call" | custom-call | flops 2264924160 | bytes 10000000 | tf_op jit(solution)/shard_map/pallas_call | solution.py:663
  (17 shorter events, 0.2 us)
Async XLA Ops:
  6.5 194.3 %all-gather.3.cloned.1.call-start = ((), (), s32[]{:S(2)}) async-start(), calls=%async_computation.3 | async-start | bytes 4456448 | tf_op jit(solution)/shard_map/all_gather | solution.py:724
  257.6 7.3 %copy-start.1 = (f32[3,1440]{1,0:T(4,128)S(1)}, f32[3,1440]{1,0:T(4,128)}, u32[]{:S(2)}) copy-start(f32[3,1440]{1,0:T(4,128)} %constant.230.clone.1) | copy-start | bytes 51844
  257.6 30.3 %all-to-all-start.2 = ((bf16[16,8,3,16,128]{4,3,2,1,0:T(8,128)(2,1)}), bf16[16,8,3,16,128]{4,3,2,1,0:T(8,128)(2,1)S(1)}, u32[]{:S(2)}, u32[]{:S(2)}) async-start(bf16[16,8,3,16,128]{4,3,2,1,0:T(8,128)(2,1)} %shard_map.76), calls=%async_computation.2 | async-start | bytes 3145728 | tf_op jit(solution)/shard_map/all_to_all | solution.py:719
  287.9 1.2 copy-start
Sparse Core Ops, SparseCore 0:
  10.7 78.3 all-gather.2

commit v3 on v2

--- a/solution.py
+++ b/solution.py
@@ -28,22 +28,10 @@
 LIMIT = 56 * 1024 * 1024
 MESH = pl.DeviceIdType.MESH
 OTHERS = (8, 7, 9, 6, 10, 5, 11, 4, 12, 3, 13, 2, 14, 1, 15)
-PLACE = (0, 1, 7, 2, 3, 4, 5, 6)
-
-
-def call(kernel, out_shape, grid, in_specs, out_specs, scratch, flops, moved):
-    return pl.pallas_call(
-        kernel,
-        out_shape=out_shape,
-        grid=grid,
-        in_specs=in_specs,
-        out_specs=out_specs,
-        scratch_shapes=scratch,
-        cost_estimate=pl.CostEstimate(flops=flops, bytes_accessed=moved, transcendentals=0),
-        compiler_params=pltpu.CompilerParams(
-            dimension_semantics=("arbitrary",) * len(grid), vmem_limit_bytes=LIMIT
-        ),
-    )
+CHUNKS = ((0, 1, 4, 7), (2, 3, 5, 6))
+SLOTS = ((0, 1, 4), (2, 3))
+BASE = {0: 0, 1: 32, 4: 64, 2: 80, 3: 112}
+SPAN = ((0, 80), (80, 64))
 
 
 def swap_blocks(xs):
@@ -120,52 +108,73 @@
     lax.fori_loop(0, NP // 16, place, 0)
 
 
-def wave_table(basis_ref, o_ref, halve):
-    width = o_ref.shape[1]
-    group_cos, group_sin = basis_ref[4, :, :width], basis_ref[5, :, :width]
-    row = lax.broadcasted_iota(jnp.int32, (8, width), 0)
-
+def wave_tile(group, basis_ref, high, low):
+    group_cos, group_sin = basis_ref[group], basis_ref[group + 1]
+    high_cos = basis_ref[2, pl.ds(high, 1), :]
+    high_sin = basis_ref[3, pl.ds(high, 1), :]
+    low_cos = basis_ref[0, low : low + 1, :]
+    low_sin = basis_ref[1, low : low + 1, :]
+    c = high_cos * low_cos - high_sin * low_sin
+    s = high_sin * low_cos + high_cos * low_sin
+    return group_cos * c - group_sin * s, -(group_sin * c + group_cos * s)
+
+
+def forward_waves(basis_ref, o_ref):
     def step(high, _):
-        high_cos = basis_ref[2, pl.ds(high, 1), :width]
-        high_sin = basis_ref[3, pl.ds(high, 1), :width]
         for low in range(8):
-            low_cos = basis_ref[0, low : low + 1, :width]
-            low_sin = basis_ref[1, low : low + 1, :width]
-            c = high_cos * low_cos - high_sin * low_sin
-            s = high_sin * low_cos + high_cos * low_sin
-            real = group_cos * c - group_sin * s
-            imag = -(group_sin * c + group_cos * s)
-            if halve and low == 0:
-                real = jnp.where(jnp.logical_and(high == 0, row == 0), 0.5 * real, real)
+            tile = wave_tile(4, basis_ref, high, low)
             offset = 8 * high + low
             start = offset // 2 % 16 * 64 + offset // 32 * 32 + low % 2 * 16
-            o_ref[pl.ds(pl.multiple_of(start, 16), 16), :] = jnp.concatenate(
-                [real, imag], axis=0
-            ).astype(BF16)
+            o_ref[pl.ds(pl.multiple_of(start, 16), 16), :] = jnp.concatenate(tile, axis=0).astype(
+                BF16
+            )
         return 0
 
     lax.fori_loop(0, 8, step, 0)
 
 
-def wave_basis(points, scale, order):
+def inverse_waves(basis_ref, o_ref):
+    row = lax.broadcasted_iota(jnp.int32, (8, NLON), 0)
+
+    def step(high, _):
+        for low in (0, 1, 4, 5):
+            for c in range(2):
+                real, imag = wave_tile(4 + 2 * c, basis_ref, high, low)
+                if low == 0 and c == 0:
+                    real = jnp.where(jnp.logical_and(high == 0, row == 0), 0.5 * real, real)
+                w = high % 4 * 2 + low // 4
+                start = c * 512 + w * 64 + high // 4 * 32 + low % 2 * 16
+                o_ref[pl.ds(pl.multiple_of(start, 16), 16), :] = jnp.concatenate(
+                    [real, imag], axis=0
+                ).astype(BF16)
+        return 0
+
+    lax.fori_loop(0, 8, step, 0)
+
+
+def wave_basis(points, scale, groups):
     count = jnp.arange(8, dtype=jnp.int32)
-    multiple = jnp.stack([count, 8 * count, 64 * jnp.array(order, jnp.int32)])
+    multiple = jnp.stack([count, 8 * count] + [jnp.array(g, jnp.int32) for g in groups])
     phase = multiple[:, :, None] * points[None, None, :] % NLON
     angle = 2.0 * jnp.pi / NLON * phase.astype(F32)
-    factor = jnp.stack([jnp.ones_like(scale), jnp.ones_like(scale), scale])[:, None, :]
+    one = jnp.ones_like(scale)
+    factor = jnp.stack([one, one] + [scale] * len(groups))[:, None, :]
     return jnp.stack([jnp.cos(angle) * factor, jnp.sin(angle) * factor], axis=1).reshape(
-        6, 8, points.shape[0]
+        -1, 8, points.shape[0]
     )
 
 
 def forward_basis():
     column = jnp.arange(NZ * NP, dtype=jnp.int32)
     n = column % NP
-    return wave_basis(column // NP * ND + n, jnp.where(n < ND, 1.0, 0.0), tuple(range(8)))
+    return wave_basis(
+        column // NP * ND + n, jnp.where(n < ND, 1.0, 0.0), [[64 * mg for mg in range(8)]]
+    )
 
 
 def inverse_basis():
-    return wave_basis(jnp.arange(NLON, dtype=jnp.int32), jnp.full((NLON,), 2.0, F32), PLACE)
+    groups = [[64 * mg + 2 * a for a in range(2) for mg in chunk] for chunk in CHUNKS]
+    return wave_basis(jnp.arange(NLON, dtype=jnp.int32), jnp.full((NLON,), 2.0, F32), groups)
 
 
 def dft_pair(x_ref, gp, table_ref, weight_ref, o_ref, acc_ref, swap_ref):
@@ -332,7 +341,7 @@
 
     pad_ref[...] = jnp.zeros_like(pad_ref)
     lax.fori_loop(0, 6, mlp_step, 0)
-    wave_table(basis_ref, table_ref, False)
+    forward_waves(basis_ref, table_ref)
     legendre(order_ref, cos_ref, log_ref, table_l, up_ref, low_ref, scale_ref, swap_l)
     for q in range(4):
         keep_table(q).start()
@@ -431,73 +440,49 @@
         all_ref[mg, rows, :] = total
 
 
-def analysis_rows(z, all_ref, o_ref):
+def analysis_rows(z, chunk, all_ref, o_ref):
     row = lax.broadcasted_iota(jnp.int32, (16, 128), 0)
     kept = []
     for t in range(2):
-        parts = [all_ref[g, pl.ds(2 * z + t, 16, stride=32), :] for g in range(8)]
-        o_ref[z, t * 16 : t * 16 + 16, :] = parts[0].astype(BF16)
-        for s in range(1, 4):
-            both = jnp.where(row < 2 * s, pltpu.roll(parts[8 - s], 2 * s, 0), parts[s])
-            o_ref[z, s * 32 + t * 16 : s * 32 + t * 16 + 16, :] = both.astype(BF16)
-        kept.append(parts[4][8:])
-    o_ref[z, 128:144, :] = jnp.concatenate(kept, axis=0).astype(BF16)
-
-
-def analysis_kernel(table_ref, x_ref, o_ref, all_ref):
-    q = pl.program_id(0)
-    for mg in range(8):
-
-        @pl.when(q == mg // 2)
-        def _(mg=mg):
-            analyse(mg, x_ref, lambda m, rows: table_ref[mg % 2 * 4 + m, rows, :], all_ref)
-
-    @pl.when(q == 3)
-    def _():
-        def place(z, _):
-            analysis_rows(z, all_ref, o_ref)
-            return 0
-
-        lax.fori_loop(0, NZ, place, 0)
-
-
-def analysis(table, fields):
-    return call(
-        analysis_kernel,
-        jax.ShapeDtypeStruct((NZ, ROWS, 128), BF16),
-        (4,),
-        [
-            pl.BlockSpec((8, MODES, JH), lambda q: (q, 0, 0)),
-            pl.BlockSpec((3, NA, 8, 16, 128), lambda q: (0, 0, 0, 0, 0)),
-        ],
-        pl.BlockSpec((NZ, ROWS, 128), lambda q: (0, 0, 0)),
-        [pltpu.VMEM((8, MODES, 128), F32)],
-        2 * 80 * 128 * JH * 256,
-        18_000_000,
-    )(table, fields)
+        where = pl.ds(2 * z + t, 16, stride=32)
+        for s in SLOTS[chunk]:
+            x = all_ref[s, where, :]
+            if s == 4:
+                kept.append(x[8:])
+                continue
+            if s:
+                x = jnp.where(row < 2 * s, pltpu.roll(all_ref[8 - s, where, :], 2 * s, 0), x)
+            start = BASE[s] + t * 16
+            o_ref[z, start : start + 16, :] = x.astype(BF16)
+    if kept:
+        o_ref[z, 64:80, :] = jnp.concatenate(kept, axis=0).astype(BF16)
 
 
 def filter_row(mg, a, t):
     if mg < 4:
-        return 32 * mg + 16 * t + a
+        return BASE[mg] + 16 * t + a
     if mg == 4:
-        return 128 + 8 * t + a - 8
-    return 32 * (8 - mg) + 16 * t + a - 2 * mg
-
-
-def filter_kernel(x_ref, w_ref, o_ref, in_ref, out_ref):
+        return BASE[4] + 8 * t + a - 8
+    return BASE[8 - mg] + 16 * t + a - 2 * mg
+
+
+def filter_chunk(chunk, x_ref, w_ref, o_ref, in_ref, out_ref):
+    begin, count = SPAN[chunk]
+
     def gather(step, _):
-        start = pl.multiple_of(step * 16, 16)
+        start = pl.multiple_of(begin + step * 16, 16)
         for h in range(2):
             xs = [x_ref[h * 8 + z, pl.ds(start, 16), :].astype(F32) for z in range(8)]
             for mr, y in enumerate(swap_blocks(xs)):
                 in_ref[h, pl.ds(start * 8 + mr, 16, stride=8), :] = y
         return 0
 
-    lax.fori_loop(0, ROWS // 16, gather, 0)
+    lax.fori_loop(0, count // 16, gather, 0)
     for a in range(16):
         for t in range(2):
-            rows = [8 * filter_row(mg, a, t) for mg in range(a // 2 + 1)]
+            rows = [8 * filter_row(mg, a, t) for mg in CHUNKS[chunk] if mg <= a // 2]
+            if not rows:
+                continue
             x = jnp.concatenate(
                 [
                     jnp.concatenate([in_ref[h, r : r + 8, :] for r in rows], axis=0)
@@ -511,45 +496,34 @@
                     out_ref[h, r : r + 8, :] = y[i * 8 : i * 8 + 8, h * 128 : h * 128 + 128]
 
     def scatter(step, _):
-        start = pl.multiple_of(step * 16, 16)
+        start = pl.multiple_of(begin + step * 16, 16)
         for h in range(2):
             xs = [out_ref[h, pl.ds(start * 8 + mr, 16, stride=8), :] for mr in range(8)]
             for z, y in enumerate(swap_blocks(xs)):
                 o_ref[h * 8 + z, pl.ds(start, 16), :] = y.astype(BF16)
         return 0
 
-    lax.fori_loop(0, ROWS // 16, scatter, 0)
-
-
-def channel_filter(coefficients, weight):
-    whole = pl.BlockSpec((NZ, ROWS, 128), lambda i: (0, 0, 0))
-    return call(
-        filter_kernel,
-        jax.ShapeDtypeStruct((NZ, ROWS, 128), BF16),
-        (1,),
-        [whole, pl.BlockSpec((NA, 2, CH, CH), lambda i: (0, 0, 0, 0))],
-        whole,
-        [pltpu.VMEM((2, ROWS * 8, 128), F32), pltpu.VMEM((2, ROWS * 8, 128), F32)],
-        2 * ROWS * 8 * CH * CH,
-        6_000_000,
-    )(coefficients, weight)
-
-
-def synthesis_rows(z, x_ref, all_ref):
+    lax.fori_loop(0, count // 16, scatter, 0)
+
+
+def synthesis_rows(z, chunk, x_ref, all_ref):
     row = lax.broadcasted_iota(jnp.int32, (16, 128), 0)
-    last = x_ref[z, 128:144, :].astype(F32)
-    for t in range(2):
-        where = pl.ds(2 * z + t, 16, stride=32)
-        all_ref[0, where, :] = x_ref[z, t * 16 : t * 16 + 16, :].astype(F32)
-        for s in range(1, 4):
-            x = x_ref[z, s * 32 + t * 16 : s * 32 + t * 16 + 16, :].astype(F32)
-            all_ref[s, where, :] = jnp.where(row >= 2 * s, x, 0.0)
-            all_ref[8 - s, where, :] = jnp.where(
-                row >= 16 - 2 * s, pltpu.roll(x, 16 - 2 * s, 0), 0.0
-            )
-        all_ref[4, where, :] = jnp.concatenate(
-            [jnp.zeros((8, 128), F32), last[t * 8 : t * 8 + 8]], axis=0
-        )
+    for s in SLOTS[chunk]:
+        for t in range(2):
+            where = pl.ds(2 * z + t, 16, stride=32)
+            if s == 4:
+                last = x_ref[z, 64:80, :].astype(F32)
+                x = jnp.concatenate([jnp.zeros((8, 128), F32), last[t * 8 : t * 8 + 8]], axis=0)
+                all_ref[4, where, :] = x
+                continue
+            start = BASE[s] + t * 16
+            x = x_ref[z, start : start + 16, :].astype(F32)
+            if s:
+                all_ref[8 - s, where, :] = jnp.where(
+                    row >= 16 - 2 * s, pltpu.roll(x, 16 - 2 * s, 0), 0.0
+                )
+                x = jnp.where(row >= 2 * s, x, 0.0)
+            all_ref[s, where, :] = x
 
 
 def synthesise(mg, table, all_ref, o_ref):
@@ -571,115 +545,256 @@
     odd = jnp.concatenate(odds, axis=0).T
     north = (even + odd).astype(BF16)
     south = (even - odd).astype(BF16)
-    place = PLACE.index(mg)
+    chunk = 0 if mg in CHUNKS[0] else 1
+    place = CHUNKS[chunk].index(mg)
     for gp in range(3):
         for a in range(8):
             rows = slice(gp * 128 + a * 16, gp * 128 + a * 16 + 16)
-            o_ref[a, place, gp] = north[rows]
-            o_ref[15 - a, place, gp] = south[rows]
-
-
-def synthesis_kernel(table_ref, x_ref, o_ref, all_ref):
-    q = pl.program_id(0)
-
-    @pl.when(q == 0)
-    def _():
-        def place(z, _):
-            synthesis_rows(z, x_ref, all_ref)
-            return 0
-
-        lax.fori_loop(0, NZ, place, 0)
-
-    for mg in range(8):
-
-        @pl.when(q == mg // 2)
-        def _(mg=mg):
-            synthesise(mg, lambda m, rows: table_ref[mg % 2 * 4 + m, rows, :], all_ref, o_ref)
-
-
-def synthesis(table, filtered):
-    return call(
-        synthesis_kernel,
-        jax.ShapeDtypeStruct((NA, 8, 3, 16, 128), BF16),
-        (4,),
-        [
-            pl.BlockSpec((8, MODES, JH), lambda q: (q, 0, 0)),
-            pl.BlockSpec((NZ, ROWS, 128), lambda q: (0, 0, 0)),
-        ],
-        pl.BlockSpec((NA, 8, 3, 16, 128), lambda q: (0, 0, 0, 0, 0)),
-        [pltpu.VMEM((8, MODES, 128), F32)],
-        2 * 80 * 128 * JH * 64,
-        18_000_000,
-    )(table, filtered)
-
-
-def inverse_pair(gp, u_ref, x_ref, table_ref, o_ref, wide_ref, rows_ref, lhs_ref, acc_ref):
-    def place(a, _):
-        wide_ref[...] = u_ref[a, :, gp].reshape(128, 128).astype(F32)
-        for gg in range(2):
-            xs = [wide_ref[pl.ds(gg * 8 + j, 8, stride=16), :] for j in range(8)]
-            for mr, y in enumerate(swap_blocks(xs)):
-                rows_ref[gg, pl.ds(pl.multiple_of(a * 64 + mr * 8, 8), 8), :] = y
-        return 0
-
-    lax.fori_loop(0, NA, place, 0)
-    for gg in range(2):
-        for k in range(8):
-            cols = slice(k * 128, (k + 1) * 128)
-            lhs_ref[gg * 128 : gg * 128 + 128, cols] = rows_ref[gg, cols, :].T.astype(BF16)
-    for part in range(2):
-        rows = slice(part * 128, part * 128 + 128)
-        acc_ref[rows, :NLON] = jnp.dot(lhs_ref[rows, :], table_ref[...], preferred_element_type=F32)
+            o_ref[chunk, gp, a, place] = north[rows]
+            o_ref[chunk, gp, 15 - a, place] = south[rows]
+
+
+def residual(gp, x_ref, acc_ref):
     row = lax.broadcasted_iota(jnp.int32, (NP, 256), 0)
     lane = lax.broadcasted_iota(jnp.int32, (NP, 256), 1)
+    acc_ref[gp] = jnp.zeros(acc_ref.shape[1:], F32)
     for z in range(NZ):
         begin = ND * z // 128 * 128
         pick = jnp.logical_and(lane == row + (ND * z - begin), row < ND)
         pick = jnp.where(pick, 1.0, 0.0).astype(BF16)
         x = jnp.concatenate([x_ref[2 * gp + gg, z].astype(F32).T for gg in range(2)], axis=0)
-        acc_ref[:, begin : begin + 256] += jnp.dot(
+        acc_ref[gp, :, begin : begin + 256] += jnp.dot(
             x.astype(BF16), pick, preferred_element_type=F32
         )
+
+
+def inverse_part(chunk, gp, u_ref, table_ref, wide_ref, rows_ref, lhs_ref, acc_ref):
+    def place(w, _):
+        wide_ref[...] = u_ref[chunk, gp, pl.ds(2 * w, 2)].reshape(128, 128).astype(F32)
+        for gg in range(2):
+            xs = [wide_ref[pl.ds(gg * 8 + j, 8, stride=16), :] for j in range(8)]
+            for mr, y in enumerate(swap_blocks(xs)):
+                rows_ref[gg, pl.ds(pl.multiple_of(w * 64 + mr * 8, 8), 8), :] = y
+        return 0
+
+    lax.fori_loop(0, 8, place, 0)
+    for gg in range(2):
+        for k in range(4):
+            cols = slice(k * 128, (k + 1) * 128)
+            lhs_ref[gg * 128 : gg * 128 + 128, cols] = rows_ref[gg, cols, :].T.astype(BF16)
+    waves = slice(chunk * 512, chunk * 512 + 512)
+    for part in range(2):
+        rows = slice(part * 128, part * 128 + 128)
+        acc_ref[gp, rows, :NLON] += jnp.dot(
+            lhs_ref[rows, :], table_ref[waves, :], preferred_element_type=F32
+        )
+
+
+def emit(gp, acc_ref, o_ref):
     for j in range(16):
 
         @pl.when(16 * gp + j < JD)
         def _(j=j):
-            o_ref[band_row(16 * gp + j)] = acc_ref[16 * j : 16 * j + 16, :NLON].astype(BF16)
-
-
-def inverse_kernel(
-    u_ref, x_ref, basis_ref, o_ref, table_ref, wide_ref, rows_ref, lhs_ref, acc_ref
+            o_ref[band_row(16 * gp + j)] = acc_ref[gp, 16 * j : 16 * j + 16, :NLON].astype(BF16)
+
+
+def backward_kernel(
+    spectrum_any,
+    legendre_any,
+    weight_any,
+    rows_any,
+    basis_ref,
+    o_ref,
+    spectrum,
+    table_l,
+    weight,
+    rows,
+    all_ref,
+    out_c,
+    got_c,
+    out_f,
+    got_f,
+    in_ref,
+    out_ref,
+    out_u,
+    got_u,
+    table_ref,
+    wide_ref,
+    rows_ref,
+    lhs_ref,
+    acc_ref,
+    load,
+    own,
+    c_send,
+    c_recv,
+    f_send,
+    f_recv,
+    u_send,
+    u_recv,
 ):
-    gp = pl.program_id(0)
-
-    @pl.when(gp == 0)
-    def _():
-        wave_table(basis_ref, table_ref, True)
-
-    inverse_pair(gp, u_ref, x_ref, table_ref, o_ref, wide_ref, rows_ref, lhs_ref, acc_ref)
-
-
-def inverse(waves, fields, basis):
-    return call(
-        inverse_kernel,
-        jax.ShapeDtypeStruct((JD, 16, NLON), BF16),
-        (3,),
-        [
-            pl.BlockSpec((NA, 8, 3, 16, 128), lambda g: (0, 0, 0, 0, 0)),
-            pl.BlockSpec((6, NZ, NP, 128), lambda g: (0, 0, 0, 0)),
-            pl.BlockSpec((6, 8, NLON), lambda g: (0, 0, 0)),
-        ],
-        pl.BlockSpec((JD, 16, NLON), lambda g: (0, 0, 0)),
-        [
+    lat = lax.axis_index("lat")
+    lon = lax.axis_index("lon")
+
+    def load_table(mg):
+        low = mg // 2 * 128
+        part = (pl.ds(4 * mg, 4), pl.ds(low, MODES - low))
+        return pltpu.make_async_copy(legendre_any.at[part], table_l.at[part], load.at[3 + mg])
+
+    load_spectrum = pltpu.make_async_copy(spectrum_any, spectrum, load.at[0])
+    load_weight = pltpu.make_async_copy(weight_any, weight, load.at[1])
+    load_rows = pltpu.make_async_copy(rows_any, rows, load.at[2])
+
+    def row_copy(chunk, out, got, send, recv):
+        part = pl.ds(*SPAN[chunk])
+
+        def copy(d):
+            return to_peer(
+                "lon",
+                d,
+                lambda peer: out.at[peer, part],
+                got.at[lon, part],
+                send.at[chunk, d],
+                recv.at[chunk, d],
+            )
+
+        return copy
+
+    def own_copy(chunk, out, got, k):
+        part = pl.ds(*SPAN[chunk])
+        return pltpu.make_async_copy(out.at[lon, part], got.at[lon, part], own.at[k, chunk])
+
+    def wave_copy(chunk, gp, d):
+        return to_peer(
+            "lat",
+            d,
+            lambda peer: out_u.at[chunk, gp, peer],
+            got_u.at[chunk, gp, lat],
+            u_send.at[chunk, gp, d],
+            u_recv.at[chunk, gp, d],
+        )
+
+    def own_wave(chunk, gp):
+        return pltpu.make_async_copy(
+            out_u.at[chunk, gp, lat], got_u.at[chunk, gp, lat], own.at[2 + chunk, gp]
+        )
+
+    def each_z(body):
+        def step(z, _):
+            body(z)
+            return 0
+
+        lax.fori_loop(0, NZ, step, 0)
+
+    def each_gp(body):
+        def step(gp, _):
+            body(gp)
+            return 0
+
+        lax.fori_loop(0, 3, step, 0)
+
+    load_spectrum.start()
+    for chunk in CHUNKS:
+        for mg in chunk:
+            load_table(mg).start()
+    load_weight.start()
+    load_rows.start()
+    greet(("lat", "lon"))
+    load_spectrum.wait()
+    for c in range(2):
+        for mg in CHUNKS[c]:
+            load_table(mg).wait()
+            analyse(mg, spectrum, lambda m, at, mg=mg: table_l[4 * mg + m, at, :], all_ref)
+        each_z(lambda z, c=c: analysis_rows(z, c, all_ref, out_c))
+        copy = row_copy(c, out_c, got_c, c_send, c_recv)
+        for d in OTHERS:
+            copy(d).start()
+        own_copy(c, out_c, got_c, 0).start()
+    inverse_waves(basis_ref, table_ref)
+    load_weight.wait()
+    load_rows.wait()
+    each_gp(lambda gp: residual(gp, rows, acc_ref))
+    for c in range(2):
+        copy = row_copy(c, out_c, got_c, c_send, c_recv)
+        own_copy(c, out_c, got_c, 0).wait()
+        for d in OTHERS:
+            copy(d).wait()
+        filter_chunk(c, got_c, weight, out_f, in_ref, out_ref)
+        copy = row_copy(c, out_f, got_f, f_send, f_recv)
+        for d in OTHERS:
+            copy(d).start()
+        own_copy(c, out_f, got_f, 1).start()
+    for c in range(2):
+        copy = row_copy(c, out_f, got_f, f_send, f_recv)
+        own_copy(c, out_f, got_f, 1).wait()
+        for d in OTHERS:
+            copy(d).wait()
+        each_z(lambda z, c=c: synthesis_rows(z, c, got_f, all_ref))
+        for mg in CHUNKS[c]:
+            synthesise(mg, lambda m, at, mg=mg: table_l[4 * mg + m, at, :], all_ref, out_u)
+
+        def send(gp, c=c):
+            for d in OTHERS:
+                wave_copy(c, gp, d).start()
+            own_wave(c, gp).start()
+
+        each_gp(send)
+    for c in range(2):
+
+        def finish(gp, c=c):
+            own_wave(c, gp).wait()
+            for d in OTHERS:
+                wave_copy(c, gp, d).wait()
+            inverse_part(c, gp, got_u, table_ref, wide_ref, rows_ref, lhs_ref, acc_ref)
+            if c == 1:
+                emit(gp, acc_ref, o_ref)
+
+        each_gp(finish)
+
+
+def backward(*operands):
+    rows = pltpu.VMEM((NZ, ROWS, 128), BF16)
+    waves = pltpu.VMEM((2, 3, NA, 4, 16, 128), BF16)
+    pairs = pltpu.SemaphoreType.DMA((2, 16))
+    return pl.pallas_call(
+        backward_kernel,
+        out_shape=jax.ShapeDtypeStruct((JD, 16, NLON), BF16),
+        in_specs=[ANY] * 4 + [VM],
+        out_specs=VM,
+        scratch_shapes=[
+            pltpu.VMEM((3, NA, 8, 16, 128), BF16),
+            pltpu.VMEM((32, MODES, JH), BF16),
+            pltpu.VMEM((NA, 2, CH, CH), BF16),
+            pltpu.VMEM((6, NZ, NP, 128), BF16),
+            pltpu.VMEM((8, MODES, 128), F32),
+            rows,
+            rows,
+            rows,
+            rows,
+            pltpu.VMEM((2, ROWS * 8, 128), F32),
+            pltpu.VMEM((2, ROWS * 8, 128), F32),
+            waves,
+            waves,
             pltpu.VMEM((KB, NLON), BF16),
             pltpu.VMEM((128, 128), F32),
-            pltpu.VMEM((2, KB, 128), F32),
-            pltpu.VMEM((256, KB), BF16),
-            pltpu.VMEM((256, 1536), F32),
+            pltpu.VMEM((2, 512, 128), F32),
+            pltpu.VMEM((256, 512), BF16),
+            pltpu.VMEM((3, 256, 1536), F32),
+            pltpu.SemaphoreType.DMA((11,)),
+            pltpu.SemaphoreType.DMA((4, 3)),
+            pairs,
+            pairs,
+            pairs,
+            pairs,
+            pltpu.SemaphoreType.DMA((2, 3, 16)),
+            pltpu.SemaphoreType.DMA((2, 3, 16)),
         ],
-        2 * KB * NLON * 768,
-        10_000_000,
-    )(waves, fields, basis)
+        cost_estimate=pl.CostEstimate(
+            flops=8_000_000_000, bytes_accessed=30_000_000, transcendentals=0
+        ),
+        compiler_params=pltpu.CompilerParams(
+            collective_id=2, has_side_effects=True, vmem_limit_bytes=LIMIT
+        ),
+    )(*operands)
 
 
 def legendre_inputs(lat_index):
@@ -715,10 +830,6 @@
     return jnp.where(local < JD, weights, 0.0).reshape(3, 1, 256)
 
 
-def exchange(x, axis):
-    return lax.all_to_all(x, axis, split_axis=0, concat_axis=0, tiled=True)
-
-
 def on_device(grid, norm_gain, mlp_in, mlp_out, filter_weight):
     lat_index = lax.axis_index("lat")
     weight = lax.all_gather(filter_weight, "lat")
@@ -731,10 +842,7 @@
         spectrum_weights(lat_index),
         *legendre_inputs(lat_index),
     )
-    coefficients = analysis(table, spectrum)
-    filtered = channel_filter(exchange(coefficients, "lon"), weight)
-    synthesized = synthesis(table, exchange(filtered, "lon"))
-    updated = inverse(exchange(synthesized, "lat"), rows, inverse_basis())
+    updated = backward(spectrum, table, weight, rows, inverse_basis())
     return updated.transpose(1, 0, 2)
 
 

time: 318 us -> 250 us (0.79)
  blocking collectives: 76.4 us -> 0 us
  Pallas kernels: 190 us -> 225 us
  waiting for transfers between devices: 22.2 us -> 0.73 us
  starting transfers between devices: 7.33 us -> 0.01 us
    all_to_all x2 -> x0, blocking collectives: 76.4 us -> none  [exchange(): return lax.all_to_all(x, axis, split_axis=0, concat_axis=0, tiled=True)]
    pallas_call x4 -> x1, Pallas kernels: 49.7 us -> 84.1 us  [backward(): pl.pallas_call(backward_kernel, out_shape=jax.ShapeDtypeStruct((JD, 16, N...]
    all_to_all x1 -> x0, waiting for transfers between devices: 21.5 us -> none  [exchange(): return lax.all_to_all(x, axis, split_axis=0, concat_axis=0, tiled=True)]
    all_to_all x1 -> x0, starting transfers between devices: 7.33 us -> none  [exchange(): return lax.all_to_all(x, axis, split_axis=0, concat_axis=0, tiled=True)]
  transfers between devices with their start and end apart: 2 -> 1, of which waited for: 1 -> 0; matrix products, arithmetic and copies ran while one was open for 2% -> 3% of each run, Pallas kernels for 47% -> 56%
where the time goes in v3:
time: 250 us
  Pallas kernels  225 us (90%)
  between operations  13.5 us (5%)
  other arithmetic  6.36 us (3%)
  local copies, waits for them, and re-layouts  4.49 us (2%)
    pallas_call x1, Pallas kernels, forward(): pl.pallas_call(forward_kernel, out_shape=(jax.ShapeDtypeStruct((6, NZ, NP...  141 us
    pallas_call x1, Pallas kernels, backward(): pl.pallas_call(backward_kernel, out_shape=jax.ShapeDtypeStruct((JD, 16, N...  84.1 us
  transfers between devices with their start and end apart: 1, of which 0 were waited for; matrix products, arithmetic and copies ran while one was open for 3% of the time, Pallas kernels for 56%

profile of v3, /device:TPU:1, one launch (start us, length us, event | category | flops | bytes accessed | tf_op | source)
XLA Modules:
  0.0 250.1 jit_solution(3493365613013576477)
XLA Ops:
  6.5 0.0 all-gather.3.cloned.1.call-start
  6.5 0.7 all-gather.3.cloned.1.call-update
  7.3 0.2 select_reduce_fusion
  7.5 0.1 mul.297
  7.7 0.1 select_log_fusion
  7.8 0.7 pad_add_fusion.1
  8.5 0.7 compare_select_fusion.1.weight_ref
  9.3 0.7 add_select_fusion.2.log_ref
  10.0 0.7 cosine_multiply_fusion.1
  10.7 0.7 pad_maximum_fusion.1
  11.4 1.6 cosine_multiply_fusion
  13.0 0.8 pad_maximum_fusion
  13.8 0.6 broadcast_in_dim.72.cos_ref
  14.4 0.7 broadcast_in_dim.70.order_ref
  15.1 140.9 %shard_map.82 = (bf16[6,16,96,128]{3,2,1,0:T(8,128)(2,1)}, bf16[3,16,8,16,128]{4,3,2,1,0:T(8,128)(2,1)}, bf16[32,512,384]{2,1,0:T(8,128)(2,1)}) custom-call(bf16[45,90,256]{2,1,0:T(8,128)(2,1)} %bitcast.12, f32[1,256]{1,0:T(1,128)} %bitcast.13, bf16[256,512]{1,0:T(8,128)(2,1)} %in_ref.1, bf16[512,256]{1,0:T(8,128)(2,1)} %out_w_ref.1, ...), custom_call_target="tpu_custom_call" | custom-call | flops 8000000000 | bytes 30000000 | tf_op jit(solution)/shard_map/pallas_call | solution.py:383
  156.0 0.0 all-gather.3.cloned.1.call-done
  156.1 84.1 %shard_map.83 = bf16[45,16,1440]{2,1,0:T(8,128)(2,1)} custom-call(bf16[3,16,8,16,128]{4,3,2,1,0:T(8,128)(2,1)} %get-tuple-element.8.spectrum_any, bf16[32,512,384]{2,1,0:T(8,128)(2,1)} %get-tuple-element.9.legendre_any, bf16[16,2,256,256]{3,2,1,0:T(8,128)(2,1)} %bitcast.11, bf16[6,16,96,128]{3,2,1,0:T(8,128)(2,1)} %get-tuple-element.10.rows_any, ...), custom_call_target="tpu_custom_call" | custom-call | flops 8000000000 | bytes 30000000 | tf_op jit(solution)/shard_map/pallas_call | solution.py:758
  240.2 3.1 %copy.10 = bf16[16,45,1440]{2,0,1:T(8,128)(2,1)} copy(bf16[16,45,1440]{2,0,1:T(8,128)(2,1)} %bitcast.8) | data formatting | bytes 4147200
  (15 shorter events, 0.2 us)
Async XLA Ops:
  6.5 149.5 %all-gather.3.cloned.1.call-start = ((), (), s32[]{:S(2)}) async-start(), calls=%async_computation | async-start | bytes 4456448 | tf_op jit(solution)/shard_map/all_gather | solution.py:835
Sparse Core Ops, SparseCore 0:
  10.7 79.9 all-gather.2

commit v4 on v3

v4 whole, which is shorter than its diff:
```python
import functools

import jax
import jax.numpy as jnp
from jax import lax
from jax.experimental import pallas as pl
from jax.experimental.pallas import tpu as pltpu
from jax.sharding import PartitionSpec as P

F32 = jnp.float32
BF16 = jnp.bfloat16

CH = 256
HID = 512
JD = 45
JP = 48
ND = 90
NP = 96
NLAT = 720
NLON = 1440
MODES = 512
NA = 16
NZ = 16
JH = NA * JP // 2
LAST = JD - 1
KB = 2 * MODES
ROWS = 144
LIMIT = 58 * 1024 * 1024
MESH = pl.DeviceIdType.MESH
OTHERS = (8, 7, 9, 6, 10, 5, 11, 4, 12, 3, 13, 2, 14, 1, 15)
CHUNKS = ((0, 4), (1, 7), (2, 6), (3, 5))
SLOTS = ((0, 4), (1,), (2,), (3,))
BASE = {0: 0, 4: 32, 1: 48, 2: 80, 3: 112}
SPAN = ((0, 48), (48, 32), (80, 32), (112, 32))
TAIL = 64
LEG = (0, 4096, 7168, 9216)


def swap_blocks(xs):
    block = lax.broadcasted_iota(jnp.int32, xs[0].shape, 1) // 16
    for bit in (1, 2, 4):
        upper = (block & bit) != 0
        new = list(xs)
        for i in range(8):
            if i & bit == 0:
                low, high = xs[i], xs[i | bit]
                new[i] = jnp.where(upper, pltpu.roll(high, 16 * bit, 1), low)
                new[i | bit] = jnp.where(upper, high, pltpu.roll(low, 128 - 16 * bit, 1))
        xs = new
    return xs


def announce(axes):
    barrier = pltpu.get_barrier_semaphore()
    for axis in axes:
        me = lax.axis_index(axis)
        for d in range(1, 16):
            pl.semaphore_signal(
                barrier, inc=1, device_id={axis: lax.rem(me + d, 16)}, device_id_type=MESH
            )
    return barrier


def to_peer(axis, d, src, dst, send, recv):
    peer = lax.rem(lax.axis_index(axis) + d, 16)
    return pltpu.make_async_remote_copy(
        src_ref=src(peer),
        dst_ref=dst,
        send_sem=send,
        recv_sem=recv,
        device_id={axis: peer},
        device_id_type=MESH,
    )


def band_row(jj):
    jj = jnp.minimum(jj, LAST)
    return jnp.where(lax.axis_index("lat") >= 8, LAST - jj, jj)


def mlp_chunk(g, x_ref, gain_ref, in_ref, out_w_ref, o_ref, pad_ref, mix_ref):
    for j in range(8):
        pad_ref[j * NP : j * NP + ND, :] = x_ref[band_row(8 * g + j)].astype(F32)
    half = 2 * NP
    for part in range(4):
        rows = slice(part * half, (part + 1) * half)
        x = pad_ref[rows, :]
        mean = jnp.mean(x, axis=1, keepdims=True)
        centered = x - mean
        spread = jnp.mean(centered * centered, axis=1, keepdims=True)
        normed = (centered * lax.rsqrt(spread + 1e-05) * gain_ref[...]).astype(BF16)
        hidden = jnp.dot(normed, in_ref[...], preferred_element_type=F32)
        hidden = jax.nn.gelu(hidden).astype(BF16)
        mixed = x + jnp.dot(hidden, out_w_ref[...], preferred_element_type=F32)
        mix_ref[0, rows, :] = mixed[:, :128]
        mix_ref[1, rows, :] = mixed[:, 128:]
    lane = lax.broadcasted_iota(jnp.int32, (16, 128), 1)
    row = lax.broadcasted_iota(jnp.int32, (16, 128), 0)
    live = lane // 16 < JD - 8 * g

    def place(step, _):
        start = pl.multiple_of(step * 16, 16)
        keep = jnp.logical_and(live, row < ND - start)
        for h in range(2):
            xs = [mix_ref[h, pl.ds(pl.multiple_of(j * NP + start, 16), 16), :] for j in range(8)]
            for z, y in enumerate(swap_blocks(xs)):
                o_ref[g, h * 8 + z, pl.ds(start, 16), :] = jnp.where(keep, y, 0.0).astype(BF16)
        return 0

    lax.fori_loop(0, NP // 16, place, 0)


def pack_tail(z, x_ref, o_ref):
    x = x_ref[5, z].astype(F32)
    low, high = x[:48], x[48:]
    block = lax.broadcasted_iota(jnp.int32, (48, 128), 1) // 16
    o_ref[z, :48, :] = jnp.where(block < 5, low, pltpu.roll(high, 80, 1)).astype(BF16)
    block = lax.broadcasted_iota(jnp.int32, (16, 128), 1) // 16
    rest = jnp.zeros((16, 128), F32)
    for b in (3, 4):
        for k in range(3):
            to = 3 * (b - 3) + k
            part = high[16 * k : 16 * k + 16]
            rest = jnp.where(block == to, pltpu.roll(part, (to - b) * 16 % 128, 1), rest)
    o_ref[z, 48:, :] = rest.astype(BF16)


def unpack_tail(z, x_ref, o_ref):
    x = x_ref[z].astype(F32)
    first, rest = x[:48], x[48:]
    block = lax.broadcasted_iota(jnp.int32, (48, 128), 1) // 16
    o_ref[5, z, :48, :] = jnp.where(block < 5, first, 0.0).astype(BF16)
    high = jnp.where(block < 3, pltpu.roll(first, 48, 1), 0.0)
    block = lax.broadcasted_iota(jnp.int32, (16, 128), 1) // 16
    for k in range(3):
        part = high[16 * k : 16 * k + 16]
        for b in (3, 4):
            held = 3 * (b - 3) + k
            part = jnp.where(block == b, pltpu.roll(rest, (b - held) * 16 % 128, 1), part)
        o_ref[5, z, 48 + 16 * k : 64 + 16 * k, :] = part.astype(BF16)


def wave_tile(group, basis_ref, high, low):
    group_cos, group_sin = basis_ref[group], basis_ref[group + 1]
    high_cos = basis_ref[2, pl.ds(high, 1), :]
    high_sin = basis_ref[3, pl.ds(high, 1), :]
    low_cos = basis_ref[0, low : low + 1, :]
    low_sin = basis_ref[1, low : low + 1, :]
    c = high_cos * low_cos - high_sin * low_sin
    s = high_sin * low_cos + high_cos * low_sin
    return group_cos * c - group_sin * s, -(group_sin * c + group_cos * s)


def forward_waves(basis_ref, o_ref):
    def step(high, _):
        for low in range(8):
            tile = wave_tile(4, basis_ref, high, low)
            offset = 8 * high + low
            start = offset // 2 % 16 * 64 + offset // 32 * 32 + low % 2 * 16
            o_ref[pl.ds(pl.multiple_of(start, 16), 16), :] = jnp.concatenate(tile, axis=0).astype(
                BF16
            )
        return 0

    lax.fori_loop(0, 8, step, 0)


def inverse_waves(basis_ref, o_ref):
    row = lax.broadcasted_iota(jnp.int32, (8, NLON), 0)

    def step(high, _):
        for low in range(2):
            for c in range(4):
                real, imag = wave_tile(4 + 2 * c, basis_ref, high, low)
                if low == 0 and c == 0:
                    real = jnp.where(jnp.logical_and(high == 0, row == 0), 0.5 * real, real)
                start = c * 256 + high % 4 * 64 + high // 4 * 32 + low * 16
                o_ref[pl.ds(pl.multiple_of(start, 16), 16), :] = jnp.concatenate(
                    [real, imag], axis=0
                ).astype(BF16)
        return 0

    lax.fori_loop(0, 8, step, 0)


def put_basis(k, o_ref, multiple, points, factor):
    phase = multiple.astype(F32) * points
    phase = phase - NLON * jnp.floor(phase * (1.0 / NLON))
    angle = 2.0 * jnp.pi / NLON * phase
    o_ref[k] = jnp.cos(angle) * factor
    o_ref[k + 1] = jnp.sin(angle) * factor


def forward_basis(o_ref):
    count = lax.broadcasted_iota(jnp.int32, (8, NZ * NP), 0)
    column = lax.broadcasted_iota(jnp.int32, (8, NZ * NP), 1).astype(F32)
    z = jnp.floor((column + 0.5) * (1.0 / NP))
    n = column - NP * z
    points = ND * z + n
    put_basis(0, o_ref, count, points, 1.0)
    put_basis(2, o_ref, 8 * count, points, 1.0)
    put_basis(4, o_ref, 64 * count, points, jnp.where(n < ND, 1.0, 0.0))


def inverse_basis(o_ref):
    count = lax.broadcasted_iota(jnp.int32, (8, NLON), 0)
    points = lax.broadcasted_iota(jnp.int32, (8, NLON), 1).astype(F32)
    put_basis(0, o_ref, count, points, 1.0)
    put_basis(2, o_ref, 8 * count, points, 1.0)
    for c, (first, second) in enumerate(CHUNKS):
        multiple = jnp.where(count % 2 == 0, 64 * first, 64 * second) + count // 2 * 2
        put_basis(4 + 2 * c, o_ref, multiple, points, 2.0)


def dft_half(g, gg, x_ref, table_ref, acc_ref):
    lat = lax.axis_index("lat")
    band = jnp.minimum(lat, 15 - lat)
    local = lax.broadcasted_iota(jnp.int32, (8, 128), 1) // 16 + 8 * g
    theta = jnp.pi * ((local + band * JD).astype(F32) + 0.5) / NLAT
    weights = jnp.pi / NLAT * jnp.sin(theta) / NLON
    weights = jnp.where(local < JD, weights, 0.0)[:1]
    x = x_ref[g].reshape(NZ * NP, 128)
    for part in range(4):
        rows = slice(part * 256, (part + 1) * 256)
        acc = jnp.dot(table_ref[rows, :], x, preferred_element_type=F32)
        acc_ref[gg, rows, :] = acc * weights


def dft_place(gp, a, acc_ref, swap_ref, o_ref):
    for gg in range(2):
        xs = [acc_ref[gg, pl.ds(pl.multiple_of(a * 64 + mr * 8, 8), 8), :] for mr in range(8)]
        for j, y in enumerate(swap_blocks(xs)):
            swap_ref[pl.ds(gg * 8 + j, 8, stride=16), :] = y
    o_ref[gp, a] = swap_ref[...].astype(BF16).reshape(8, 16, 128)


def legendre_orders(q, width):
    row = lax.broadcasted_iota(jnp.int32, (8, width), 0)
    order = 128 * q + row // 4 * 64 + row // 2 % 2 * 32 + row % 2
    return (order + 2 * lax.axis_index("lat")).astype(F32)


def legendre_start(cos_ref, scale_ref):
    column = lax.broadcasted_iota(jnp.int32, (8, JH), 1)
    local = column // 128 * 16 + column % 16
    theta = jnp.pi * ((column // 16 % 8 * JD + local).astype(F32) + 0.5) / NLAT
    real = local < JD
    cos_ref[...] = jnp.where(real, jnp.cos(theta), 0.0)
    log_sine = jnp.log(jnp.where(real, jnp.sin(theta), 1.0))
    counts = (lax.broadcasted_iota(jnp.int32, (8, MODES), 1) + 1).astype(F32)
    ratios = jnp.log((2.0 * counts - 1.0) / (2.0 * counts))
    for q in range(4):
        partial_log = jnp.sum(
            jnp.where(counts <= legendre_orders(q, MODES), ratios, 0.0), axis=1, keepdims=True
        )
        order = legendre_orders(q, JH)
        start_log = order * log_sine + 0.5 * jnp.log(order + 0.5) + 0.5 * partial_log
        scale_ref[q] = jnp.where(real, start_log, -1e9)


def legendre_rows(mg, m, rows):
    q = mg // 2
    base = LEG[q] + (mg % 2 * 4 + m) * (MODES - 128 * q) - 128 * q
    return slice(base + rows.start, base + rows.stop)


def legendre_group(q, i, cos_ref, o_ref, up_ref, low_ref, scale_ref, swap_ref):
    order = legendre_orders(q, 128)
    degree = lax.broadcasted_iota(jnp.int32, (8, 128), 1) + 16 * i
    degree = degree.astype(F32)
    active = degree > order
    second = degree > order + 1.0
    grow = jnp.sqrt(
        jnp.where(active, 4.0 * degree * degree - 1.0, 0.0)
        / jnp.where(active, degree * degree - order * order, 1.0)
    )
    before = degree - 1.0
    damp = grow * jnp.sqrt(
        jnp.where(second, before * before - order * order, 0.0)
        / jnp.where(second, 4.0 * before * before - 1.0, 1.0)
    )
    first = jnp.where(degree == order, 1.0, 0.0)
    up, low, scale_log = up_ref[q], low_ref[q], scale_ref[q]
    root = jnp.exp(0.5 * scale_log)
    cosine = cos_ref[...]
    for s in range(16):
        a = jnp.broadcast_to(grow[:, s : s + 1], (8, JH))
        b = jnp.broadcast_to(damp[:, s : s + 1], (8, JH))
        e = jnp.broadcast_to(first[:, s : s + 1], (8, JH))
        fresh = a * (cosine * up) - b * low + e
        low = up
        up = fresh
        value = fresh * root * root
        for k in range(3):
            swap_ref[q, k, s * 8 : s * 8 + 8, :] = value[:, k * 128 : k * 128 + 128]
    largest = jnp.maximum(jnp.abs(up), jnp.abs(low))
    largest = jnp.where(largest > 0.0, largest, 1.0)
    up_ref[q] = up / largest
    low_ref[q] = low / largest
    scale_ref[q] = scale_log + jnp.log(largest)
    for m in range(8):
        base = LEG[q] + m * (MODES - 128 * q) - 128 * q
        start = pl.multiple_of(base + i * 16, 16)
        for k in range(3):
            o_ref[pl.ds(start, 16), k * 128 : k * 128 + 128] = swap_ref[
                q, k, pl.ds(m, 16, stride=8), :
            ].astype(BF16)


def legendre(cos_ref, o_ref, up_ref, low_ref, scale_ref, swap_ref):
    up_ref[...] = jnp.zeros_like(up_ref)
    low_ref[...] = jnp.zeros_like(low_ref)
    legendre_start(cos_ref, scale_ref)
    for stage in range(4):

        def step(i, _, stage=stage):
            for q in range(stage + 1):
                legendre_group(q, i, cos_ref, o_ref, up_ref, low_ref, scale_ref, swap_ref)
            return 0

        lax.fori_loop(8 * stage, 8 * stage + 8, step, 0)


def analyse(mg, x_ref, table_ref, all_ref):
    north, south = [], []
    for gp in range(3):
        north.append(x_ref[gp, :8, mg].reshape(128, 128).astype(F32))
        south.append(jnp.concatenate([x_ref[gp, 15 - a, mg] for a in range(8)], axis=0).astype(F32))
    north = jnp.concatenate(north, axis=0)
    south = jnp.concatenate(south, axis=0)
    both = jnp.concatenate([north + south, north - south], axis=1).astype(BF16)
    block = lax.broadcasted_iota(jnp.int32, (128, 128), 1) // 32
    odd = lax.broadcasted_iota(jnp.int32, (128, 128), 0) % 2 == 1
    for lb in range(mg // 2, 4):
        rows = slice(lb * 128, lb * 128 + 128)
        total = jnp.zeros((128, 128), F32)
        for m in range(4):
            entries = table_ref[legendre_rows(mg, m, rows), :]
            part = jnp.dot(entries, both, preferred_element_type=F32)
            first, second = part[:, :128], part[:, 128:]
            if m % 2:
                first, second = second, first
            total = jnp.where(block == m, jnp.where(odd, second, first), total)
        all_ref[mg, rows, :] = total


def analysis_rows(z, chunk, all_ref, o_ref):
    row = lax.broadcasted_iota(jnp.int32, (16, 128), 0)
    kept = []
    for t in range(2):
        where = pl.ds(2 * z + t, 16, stride=32)
        for s in SLOTS[chunk]:
            x = all_ref[s, where, :]
            if s == 4:
                kept.append(x[8:])
                continue
            if s:
                x = jnp.where(row < 2 * s, pltpu.roll(all_ref[8 - s, where, :], 2 * s, 0), x)
            start = BASE[s] + t * 16
            o_ref[z, start : start + 16, :] = x.astype(BF16)
    if kept:
        o_ref[z, 32:48, :] = jnp.concatenate(kept, axis=0).astype(BF16)


def filter_row(mg, a, t):
    if mg < 4:
        return BASE[mg] + 16 * t + a
    if mg == 4:
        return BASE[4] + 8 * t + a - 8
    return BASE[8 - mg] + 16 * t + a - 2 * mg


def filter_chunk(chunk, x_ref, w_ref, o_ref, in_ref, out_ref):
    begin, count = SPAN[chunk]

    def gather(step, _):
        start = pl.multiple_of(begin + step * 16, 16)
        for h in range(2):
            xs = [x_ref[h * 8 + z, pl.ds(start, 16), :].astype(F32) for z in range(8)]
            for mr, y in enumerate(swap_blocks(xs)):
                in_ref[h, pl.ds(start * 8 + mr, 16, stride=8), :] = y
        return 0

    lax.fori_loop(0, count // 16, gather, 0)
    for a in range(16):
        for t in range(2):
            rows = [8 * filter_row(mg, a, t) for mg in CHUNKS[chunk] if mg <= a // 2]
            if not rows:
                continue
            x = jnp.concatenate(
                [
                    jnp.concatenate([in_ref[h, r : r + 8, :] for r in rows], axis=0)
                    for h in range(2)
                ],
                axis=1,
            ).astype(BF16)
            y = jnp.dot(x, w_ref[a, t], preferred_element_type=F32)
            for i, r in enumerate(rows):
                for h in range(2):
                    out_ref[h, r : r + 8, :] = y[i * 8 : i * 8 + 8, h * 128 : h * 128 + 128]

    def scatter(step, _):
        start = pl.multiple_of(begin + step * 16, 16)
        for h in range(2):
            xs = [out_ref[h, pl.ds(start * 8 + mr, 16, stride=8), :] for mr in range(8)]
            for z, y in enumerate(swap_blocks(xs)):
                o_ref[h * 8 + z, pl.ds(start, 16), :] = y.astype(BF16)
        return 0

    lax.fori_loop(0, count // 16, scatter, 0)


def synthesis_rows(z, chunk, x_ref, all_ref):
    row = lax.broadcasted_iota(jnp.int32, (16, 128), 0)
    for s in SLOTS[chunk]:
        for t in range(2):
            where = pl.ds(2 * z + t, 16, stride=32)
            if s == 4:
                last = x_ref[z, 32:48, :].astype(F32)
                x = jnp.concatenate([jnp.zeros((8, 128), F32), last[t * 8 : t * 8 + 8]], axis=0)
                all_ref[4, where, :] = x
                continue
            start = BASE[s] + t * 16
            x = x_ref[z, start : start + 16, :].astype(F32)
            if s:
                all_ref[8 - s, where, :] = jnp.where(
                    row >= 16 - 2 * s, pltpu.roll(x, 16 - 2 * s, 0), 0.0
                )
                x = jnp.where(row >= 2 * s, x, 0.0)
            all_ref[s, where, :] = x


def synthesise(chunk, place, table_ref, all_ref, o_ref):
    mg = CHUNKS[chunk][place]
    low = mg // 2 * 128
    block = lax.broadcasted_iota(jnp.int32, (MODES - low, 128), 1) // 32
    row = lax.broadcasted_iota(jnp.int32, (MODES - low, 128), 0)
    same = (block + row) % 2 == 0
    x = all_ref[mg, low:, :]
    even = jnp.where(same, x, 0.0).T.astype(BF16)
    odd = jnp.where(same, 0.0, x).T.astype(BF16)
    evens, odds = [], []
    for m in range(4):
        rows = slice(m * 32, m * 32 + 32)
        both = jnp.concatenate([even[rows], odd[rows]], axis=0)
        entries = table_ref[legendre_rows(mg, m, slice(low, MODES)), :]
        part = jnp.dot(both, entries, preferred_element_type=F32)
        evens.append(part[:32])
        odds.append(part[32:])
    even = jnp.concatenate(evens, axis=0).T
    odd = jnp.concatenate(odds, axis=0).T
    north = (even + odd).astype(BF16)
    south = (even - odd).astype(BF16)
    for gp in range(3):
        for a in range(8):
            rows = slice(gp * 128 + a * 16, gp * 128 + a * 16 + 16)
            o_ref[chunk, a, gp, place] = north[rows]
            o_ref[chunk, 15 - a, gp, place] = south[rows]


def residual(gp, x_ref, acc_ref):
    row = lax.broadcasted_iota(jnp.int32, (NP, 256), 0)
    lane = lax.broadcasted_iota(jnp.int32, (NP, 256), 1)
    acc_ref[gp] = jnp.zeros(acc_ref.shape[1:], F32)
    for z in range(NZ):
        begin = ND * z // 128 * 128
        pick = jnp.logical_and(lane == row + (ND * z - begin), row < ND)
        pick = jnp.where(pick, 1.0, 0.0).astype(BF16)
        x = jnp.concatenate([x_ref[2 * gp + gg, z].astype(F32).T for gg in range(2)], axis=0)
        acc_ref[gp, :, begin : begin + 256] += jnp.dot(
            x.astype(BF16), pick, preferred_element_type=F32
        )


def inverse_part(chunk, gp, u_ref, table_ref, wide_ref, rows_ref, lhs_ref, acc_ref):
    def place(w, _):
        wide_ref[...] = u_ref[chunk, pl.ds(4 * w, 4), gp].reshape(128, 128).astype(F32)
        for gg in range(2):
            xs = [wide_ref[pl.ds(gg * 8 + j, 8, stride=16), :] for j in range(8)]
            for mr, y in enumerate(swap_blocks(xs)):
                rows_ref[gg, pl.ds(pl.multiple_of(w * 64 + mr * 8, 8), 8), :] = y
        return 0

    lax.fori_loop(0, 4, place, 0)
    for gg in range(2):
        for k in range(2):
            cols = slice(k * 128, (k + 1) * 128)
            lhs_ref[gg * 128 : gg * 128 + 128, cols] = rows_ref[gg, cols, :].T.astype(BF16)
    waves = slice(chunk * 256, chunk * 256 + 256)
    for part in range(2):
        rows = slice(part * 128, part * 128 + 128)
        acc_ref[gp, rows, :NLON] += jnp.dot(
            lhs_ref[rows, :], table_ref[waves, :], preferred_element_type=F32
        )


def emit(gp, acc_ref, o_ref):
    for j in range(16):

        @pl.when(16 * gp + j < JD)
        def _(j=j):
            o_ref[band_row(16 * gp + j)] = acc_ref[gp, 16 * j : 16 * j + 16, :NLON].astype(BF16)


VM = pl.BlockSpec(memory_space=pltpu.VMEM)
ANY = pl.BlockSpec(memory_space=pl.ANY)
SCRATCH = {
    "points": pltpu.VMEM((JD, ND, CH), BF16),
    "pad": pltpu.VMEM((8 * NP, CH), F32),
    "mix": pltpu.VMEM((2, 8 * NP, 128), F32),
    "out_rows": pltpu.VMEM((6, NZ, NP, 128), BF16),
    "got_rows": pltpu.VMEM((6, NZ, NP, 128), BF16),
    "out_tail": pltpu.VMEM((NZ, TAIL, 128), BF16),
    "got_tail": pltpu.VMEM((NZ, TAIL, 128), BF16),
    "basis_f": pltpu.VMEM((6, 8, NZ * NP), F32),
    "basis_i": pltpu.VMEM((12, 8, NLON), F32),
    "waves_f": pltpu.VMEM((KB, NZ * NP), BF16),
    "waves_i": pltpu.VMEM((KB, NLON), BF16),
    "acc_f": pltpu.VMEM((2, KB, 128), F32),
    "swap_f": pltpu.VMEM((128, 128), F32),
    "out_spectrum": pltpu.VMEM((3, NA, 8, 16, 128), BF16),
    "got_spectrum": pltpu.VMEM((3, NA, 8, 16, 128), BF16),
    "table": pltpu.VMEM((10240, JH), BF16),
    "cosine": pltpu.VMEM((8, JH), F32),
    "up": pltpu.VMEM((4, 8, JH), F32),
    "low": pltpu.VMEM((4, 8, JH), F32),
    "scale": pltpu.VMEM((4, 8, JH), F32),
    "swap_l": pltpu.VMEM((4, 3, 128, 128), F32),
    "weight": pltpu.VMEM((NA, 2, CH, CH), BF16),
    "every": pltpu.VMEM((8, MODES, 128), F32),
    "out_c": pltpu.VMEM((NZ, ROWS, 128), BF16),
    "got_c": pltpu.VMEM((NZ, ROWS, 128), BF16),
    "out_f": pltpu.VMEM((NZ, ROWS, 128), BF16),
    "got_f": pltpu.VMEM((NZ, ROWS, 128), BF16),
    "wide_in": pltpu.VMEM((2, ROWS * 8, 128), F32),
    "wide_out": pltpu.VMEM((2, ROWS * 8, 128), F32),
    "out_u": pltpu.VMEM((4, NA, 3, 2, 16, 128), BF16),
    "got_u": pltpu.VMEM((4, NA, 3, 2, 16, 128), BF16),
    "wide_u": pltpu.VMEM((128, 128), F32),
    "rows_u": pltpu.VMEM((2, 256, 128), F32),
    "lhs_u": pltpu.VMEM((256, 256), BF16),
    "acc_u": pltpu.VMEM((3, 256, 1536), F32),
    "load": pltpu.SemaphoreType.DMA((2,)),
    "own": pltpu.SemaphoreType.DMA((5, 6)),
    "r_send": pltpu.SemaphoreType.DMA((6, 16)),
    "r_recv": pltpu.SemaphoreType.DMA((6, 16)),
    "s_send": pltpu.SemaphoreType.DMA((3, 16)),
    "s_recv": pltpu.SemaphoreType.DMA((3, 16)),
    "w_send": pltpu.SemaphoreType.DMA((16,)),
    "w_recv": pltpu.SemaphoreType.DMA((16,)),
    "c_send": pltpu.SemaphoreType.DMA((4, 16)),
    "c_recv": pltpu.SemaphoreType.DMA((4, 16)),
    "f_send": pltpu.SemaphoreType.DMA((4, 16)),
    "f_recv": pltpu.SemaphoreType.DMA((4, 16)),
    "u_send": pltpu.SemaphoreType.DMA((4, 16)),
    "u_recv": pltpu.SemaphoreType.DMA((4, 16)),
}


def each(low, high, body):
    def step(i, _):
        body(i)
        return 0

    lax.fori_loop(low, high, step, 0)


def block_kernel(points_any, gain_ref, in_ref, out_ref, weight_any, o_ref, *scratch):
    v = dict(zip(SCRATCH, scratch))
    lat = lax.axis_index("lat")
    lon = lax.axis_index("lon")
    own = v["own"]

    def rows_copy(g, d):
        return to_peer(
            "lon",
            d,
            lambda peer: v["out_rows"].at[g, peer],
            v["got_rows"].at[g, lon],
            v["r_send"].at[g, d],
            v["r_recv"].at[g, d],
        )

    def own_rows(g):
        return pltpu.make_async_copy(
            v["out_rows"].at[g, lon], v["got_rows"].at[g, lon], own.at[0, g]
        )

    def tail_copy(d):
        return to_peer(
            "lon",
            d,
            lambda peer: v["out_tail"].at[peer],
            v["got_tail"].at[lon],
            v["r_send"].at[5, d],
            v["r_recv"].at[5, d],
        )

    own_tail = pltpu.make_async_copy(v["out_tail"].at[lon], v["got_tail"].at[lon], own.at[0, 5])

    def spectrum_copy(gp, d):
        return to_peer(
            "lat",
            d,
            lambda peer: v["out_spectrum"].at[gp, peer],
            v["got_spectrum"].at[gp, lat],
            v["s_send"].at[gp, d],
            v["s_recv"].at[gp, d],
        )

    def own_spectrum(gp):
        return pltpu.make_async_copy(
            v["out_spectrum"].at[gp, lat], v["got_spectrum"].at[gp, lat], own.at[1, gp]
        )

    def weight_copy(d):
        return to_peer(
            "lat",
            d,
            lambda peer: weight_any,
            v["weight"].at[lat],
            v["w_send"].at[d],
            v["w_recv"].at[d],
        )

    own_weight = pltpu.make_async_copy(weight_any, v["weight"].at[lat], v["load"].at[1])

    def mode_copy(c, name, d):
        part = pl.ds(*SPAN[c])
        return to_peer(
            "lon",
            d,
            lambda peer: v["out_" + name].at[peer, part],
            v["got_" + name].at[lon, part],
            v[name + "_send"].at[c, d],
            v[name + "_recv"].at[c, d],
        )

    def own_modes(c, name):
        part = pl.ds(*SPAN[c])
        return pltpu.make_async_copy(
            v["out_" + name].at[lon, part],
            v["got_" + name].at[lon, part],
            own.at[2 if name == "c" else 3, c],
        )

    def u_copy(c, d):
        return to_peer(
            "lat",
            d,
            lambda peer: v["out_u"].at[c, peer],
            v["got_u"].at[c, lat],
            v["u_send"].at[c, d],
            v["u_recv"].at[c, d],
        )

    def own_u(c):
        return pltpu.make_async_copy(v["out_u"].at[c, lat], v["got_u"].at[c, lat], own.at[4, c])

    def mlp_step(g):
        mlp_chunk(
            g, v["points"], gain_ref, in_ref, out_ref, v["out_rows"], v["pad"], v["mix"]
        )

    def send_rows(g):
        for d in OTHERS:
            rows_copy(g, d).start()
        own_rows(g).start()

    def dft_step(g, gg):
        dft_half(g, gg, v["got_rows"], v["waves_f"], v["acc_f"])

    def got_rows(g):
        own_rows(g).wait()
        for d in OTHERS:
            rows_copy(g, d).wait_recv()

    def send_spectrum(gp):
        def one(d):
            peer = lax.rem(lat + d, 16)
            dft_place(gp, peer, v["acc_f"], v["swap_f"], v["out_spectrum"])
            spectrum_copy(gp, d).start()

        each(1, 16, one)
        dft_place(gp, lat, v["acc_f"], v["swap_f"], v["out_spectrum"])
        own_spectrum(gp).start()

    load_points = pltpu.make_async_copy(points_any, v["points"], v["load"].at[0])
    load_points.start()
    barrier = announce(("lat", "lon"))
    v["pad"][...] = jnp.zeros_like(v["pad"])
    load_points.wait()
    mlp_step(0)
    pl.semaphore_wait(barrier, 30)
    send_rows(0)

    def mlp_more(g):
        mlp_step(g)

        @pl.when(g < 5)
        def _():
            send_rows(g)

    each(1, 6, mlp_more)
    each(0, NZ, lambda z: pack_tail(z, v["out_rows"], v["out_tail"]))
    for d in OTHERS:
        tail_copy(d).start()
    own_tail.start()
    for d in OTHERS:
        weight_copy(d).start()
    own_weight.start()

    forward_basis(v["basis_f"])
    forward_waves(v["basis_f"], v["waves_f"])
    legendre(v["cosine"], v["table"], v["up"], v["low"], v["scale"], v["swap_l"])
    inverse_basis(v["basis_i"])
    inverse_waves(v["basis_i"], v["waves_i"])

    def pair(gp):
        for gg in range(2):
            got_rows(2 * gp + gg)
            dft_step(2 * gp + gg, gg)
        send_spectrum(gp)
        residual(gp, v["got_rows"], v["acc_u"])

    each(0, 2, pair)
    got_rows(4)
    dft_step(4, 0)
    own_tail.wait()
    for d in OTHERS:
        tail_copy(d).wait_recv()
    each(0, NZ, lambda z: unpack_tail(z, v["got_tail"], v["got_rows"]))
    dft_step(5, 1)
    send_spectrum(2)
    residual(2, v["got_rows"], v["acc_u"])

    def got_spectrum(gp):
        own_spectrum(gp).wait()
        for d in OTHERS:
            spectrum_copy(gp, d).wait()

    each(0, 3, got_spectrum)
    for c in range(4):
        for mg in CHUNKS[c]:
            analyse(mg, v["got_spectrum"], v["table"], v["every"])
        each(0, NZ, lambda z, c=c: analysis_rows(z, c, v["every"], v["out_c"]))
        for d in OTHERS:
            mode_copy(c, "c", d).start()
        own_modes(c, "c").start()
    own_weight.wait()
    for d in OTHERS:
        weight_copy(d).wait()
    for c in range(4):
        own_modes(c, "c").wait()
        for d in OTHERS:
            mode_copy(c, "c", d).wait()
        filter_chunk(c, v["got_c"], v["weight"], v["out_f"], v["wide_in"], v["wide_out"])
        for d in OTHERS:
            mode_copy(c, "f", d).start()
        own_modes(c, "f").start()

    def inverse_step(c, last):
        own_u(c).wait()
        for d in OTHERS:
            u_copy(c, d).wait()

        def one(gp):
            inverse_part(
                c, gp, v["got_u"], v["waves_i"], v["wide_u"], v["rows_u"], v["lhs_u"], v["acc_u"]
            )
            if last:
                emit(gp, v["acc_u"], o_ref)

        each(0, 3, one)

    for c in range(4):
        own_modes(c, "f").wait()
        for d in OTHERS:
            mode_copy(c, "f", d).wait()
        each(0, NZ, lambda z, c=c: synthesis_rows(z, c, v["got_f"], v["every"]))
        for place in range(2):
            synthesise(c, place, v["table"], v["every"], v["out_u"])
        for d in OTHERS:
            u_copy(c, d).start()
        own_u(c).start()
        if c >= 1:
            inverse_step(c - 1, False)

    def rows_sent(g):
        for d in OTHERS:
            rows_copy(g, d).wait_send()

    each(0, 5, rows_sent)
    for d in OTHERS:
        tail_copy(d).wait_send()
    inverse_step(3, True)


def on_device(grid, norm_gain, mlp_in, mlp_out, filter_weight):
    updated = pl.pallas_call(
        block_kernel,
        out_shape=jax.ShapeDtypeStruct((JD, 16, NLON), BF16),
        in_specs=[ANY, VM, VM, VM, ANY],
        out_specs=VM,
        scratch_shapes=list(SCRATCH.values()),
        cost_estimate=pl.CostEstimate(
            flops=20_000_000_000, bytes_accessed=10_000_000, transcendentals=0
        ),
        compiler_params=pltpu.CompilerParams(
            collective_id=1, has_side_effects=True, vmem_limit_bytes=LIMIT
        ),
    )(grid.transpose(1, 2, 0), norm_gain.reshape(1, CH), mlp_in, mlp_out, filter_weight)
    return updated.transpose(1, 0, 2)


def solution(mesh):
    return jax.shard_map(
        on_device,
        mesh=mesh,
        in_specs=(P("batch", "lat", "lon"), P(), P(), P(), P(("lat", "lon"), None, None)),
        out_specs=P(("batch", "lon"), "lat", None),
        check_vma=False,
    )
```

time: 250 us -> 208 us (0.83)
  Pallas kernels: 225 us -> 205 us
  between operations: 13.5 us -> 0.01 us
  other arithmetic: 6.36 us -> 0 us
    pallas_call x2 -> x1, Pallas kernels: 225 us -> 205 us  [on_device(): pl.pallas_call(block_kernel, out_shape=jax.ShapeDtypeStruct((JD, 16, NLON...]
  transfers between devices with their start and end apart: 1 -> 0, of which waited for: 0 -> 0; matrix products, arithmetic and copies ran while one was open for 3% -> 0% of each run, Pallas kernels for 56% -> 0%
where the time goes in v4:
time: 208 us
  Pallas kernels  205 us (99%)
  local copies, waits for them, and re-layouts  3.12 us (2%)
    pallas_call x1, Pallas kernels, on_device(): pl.pallas_call(block_kernel, out_shape=jax.ShapeDtypeStruct((JD, 16, NLON...  205 us

profile of v4, /device:TPU:1, one launch (start us, length us, event | category | flops | bytes accessed | tf_op | source)
XLA Modules:
  0.0 208.2 jit_solution(5280202064903847243)
XLA Ops:
  0.0 205.1 %shard_map.55 = bf16[45,16,1440]{2,1,0:T(8,128)(2,1)} custom-call(bf16[45,90,256]{2,1,0:T(8,128)(2,1)} %bitcast.4, f32[1,256]{1,0:T(1,128)} %bitcast.5, bf16[256,512]{1,0:T(8,128)(2,1)} %in_ref.1, bf16[512,256]{1,0:T(8,128)(2,1)} %out_ref.1, bf16[2,256,256]{2,1,0:T(8,128)(2,1)} %weight_any.1), custom_call_target="tpu_custom_call" | custom-call | flops 20000000000 | bytes 10000000 | tf_op jit(solution)/shard_map/pallas_call | solution.py:800
  205.1 3.1 %copy.7 = bf16[16,45,1440]{2,0,1:T(8,128)(2,1)} copy(bf16[16,45,1440]{2,0,1:T(8,128)(2,1)} %bitcast.3) | data formatting | bytes 4147200

commit v5 on v4

--- a/solution.py
+++ b/solution.py
@@ -28,10 +28,10 @@
 LIMIT = 58 * 1024 * 1024
 MESH = pl.DeviceIdType.MESH
 OTHERS = (8, 7, 9, 6, 10, 5, 11, 4, 12, 3, 13, 2, 14, 1, 15)
-CHUNKS = ((0, 4), (1, 7), (2, 6), (3, 5))
-SLOTS = ((0, 4), (1,), (2,), (3,))
-BASE = {0: 0, 4: 32, 1: 48, 2: 80, 3: 112}
-SPAN = ((0, 48), (48, 32), (80, 32), (112, 32))
+CHUNKS = ((3, 5), (0, 4), (1, 7), (2, 6))
+SLOTS = ((3,), (0, 4), (1,), (2,))
+BASE = {3: 0, 0: 32, 4: 64, 1: 80, 2: 112}
+SPAN = ((0, 32), (32, 48), (80, 32), (112, 32))
 TAIL = 64
 LEG = (0, 4096, 7168, 9216)
 
@@ -172,7 +172,7 @@
         for low in range(2):
             for c in range(4):
                 real, imag = wave_tile(4 + 2 * c, basis_ref, high, low)
-                if low == 0 and c == 0:
+                if low == 0 and c == 1:
                     real = jnp.where(jnp.logical_and(high == 0, row == 0), 0.5 * real, real)
                 start = c * 256 + high % 4 * 64 + high // 4 * 32 + low * 16
                 o_ref[pl.ds(pl.multiple_of(start, 16), 16), :] = jnp.concatenate(
@@ -212,7 +212,7 @@
         put_basis(4 + 2 * c, o_ref, multiple, points, 2.0)
 
 
-def dft_half(g, gg, x_ref, table_ref, acc_ref):
+def dft(g, x_ref, table_ref, acc_ref):
     lat = lax.axis_index("lat")
     band = jnp.minimum(lat, 15 - lat)
     local = lax.broadcasted_iota(jnp.int32, (8, 128), 1) // 16 + 8 * g
@@ -223,15 +223,14 @@
     for part in range(4):
         rows = slice(part * 256, (part + 1) * 256)
         acc = jnp.dot(table_ref[rows, :], x, preferred_element_type=F32)
-        acc_ref[gg, rows, :] = acc * weights
-
-
-def dft_place(gp, a, acc_ref, swap_ref, o_ref):
-    for gg in range(2):
-        xs = [acc_ref[gg, pl.ds(pl.multiple_of(a * 64 + mr * 8, 8), 8), :] for mr in range(8)]
-        for j, y in enumerate(swap_blocks(xs)):
-            swap_ref[pl.ds(gg * 8 + j, 8, stride=16), :] = y
-    o_ref[gp, a] = swap_ref[...].astype(BF16).reshape(8, 16, 128)
+        acc_ref[rows, :] = acc * weights
+
+
+def dft_place(g, a, acc_ref, swap_ref, o_ref):
+    xs = [acc_ref[pl.ds(pl.multiple_of(a * 64 + mr * 8, 8), 8), :] for mr in range(8)]
+    for j, y in enumerate(swap_blocks(xs)):
+        swap_ref[pl.ds(j, 8, stride=8), :] = y
+    o_ref[g, a] = swap_ref[...].astype(BF16)
 
 
 def legendre_orders(q, width):
@@ -242,8 +241,8 @@
 
 def legendre_start(cos_ref, scale_ref):
     column = lax.broadcasted_iota(jnp.int32, (8, JH), 1)
-    local = column // 128 * 16 + column % 16
-    theta = jnp.pi * ((column // 16 % 8 * JD + local).astype(F32) + 0.5) / NLAT
+    local = column // 64 * 8 + column % 8
+    theta = jnp.pi * ((column // 8 % 8 * JD + local).astype(F32) + 0.5) / NLAT
     real = local < JD
     cos_ref[...] = jnp.where(real, jnp.cos(theta), 0.0)
     log_sine = jnp.log(jnp.where(real, jnp.sin(theta), 1.0))
@@ -323,9 +322,12 @@
 
 def analyse(mg, x_ref, table_ref, all_ref):
     north, south = [], []
-    for gp in range(3):
-        north.append(x_ref[gp, :8, mg].reshape(128, 128).astype(F32))
-        south.append(jnp.concatenate([x_ref[gp, 15 - a, mg] for a in range(8)], axis=0).astype(F32))
+    start = mg // 2 * 16
+    part = slice(mg % 2 * 8, mg % 2 * 8 + 8)
+    for g in range(6):
+        x = x_ref[g, :, start : start + 16, :].astype(F32)[:, part]
+        north.append(x[:8].reshape(64, 128))
+        south += [x[15 - a] for a in range(8)]
     north = jnp.concatenate(north, axis=0)
     south = jnp.concatenate(south, axis=0)
     both = jnp.concatenate([north + south, north - south], axis=1).astype(BF16)
@@ -359,7 +361,7 @@
             start = BASE[s] + t * 16
             o_ref[z, start : start + 16, :] = x.astype(BF16)
     if kept:
-        o_ref[z, 32:48, :] = jnp.concatenate(kept, axis=0).astype(BF16)
+        o_ref[z, 64:80, :] = jnp.concatenate(kept, axis=0).astype(BF16)
 
 
 def filter_row(mg, a, t):
@@ -416,7 +418,7 @@
         for t in range(2):
             where = pl.ds(2 * z + t, 16, stride=32)
             if s == 4:
-                last = x_ref[z, 32:48, :].astype(F32)
+                last = x_ref[z, 64:80, :].astype(F32)
                 x = jnp.concatenate([jnp.zeros((8, 128), F32), last[t * 8 : t * 8 + 8]], axis=0)
                 all_ref[4, where, :] = x
                 continue
@@ -449,13 +451,15 @@
         odds.append(part[32:])
     even = jnp.concatenate(evens, axis=0).T
     odd = jnp.concatenate(odds, axis=0).T
-    north = (even + odd).astype(BF16)
-    south = (even - odd).astype(BF16)
+    north = even + odd
+    south = even - odd
     for gp in range(3):
         for a in range(8):
-            rows = slice(gp * 128 + a * 16, gp * 128 + a * 16 + 16)
-            o_ref[chunk, a, gp, place] = north[rows]
-            o_ref[chunk, 15 - a, gp, place] = south[rows]
+            first = gp * 128 + a * 8
+            for x, to in ((north, a), (south, 15 - a)):
+                o_ref[chunk, to, gp, place] = jnp.concatenate(
+                    [x[first : first + 8], x[first + 64 : first + 72]], axis=0
+                ).astype(BF16)
 
 
 def residual(gp, x_ref, acc_ref):
@@ -516,10 +520,10 @@
     "basis_i": pltpu.VMEM((12, 8, NLON), F32),
     "waves_f": pltpu.VMEM((KB, NZ * NP), BF16),
     "waves_i": pltpu.VMEM((KB, NLON), BF16),
-    "acc_f": pltpu.VMEM((2, KB, 128), F32),
-    "swap_f": pltpu.VMEM((128, 128), F32),
-    "out_spectrum": pltpu.VMEM((3, NA, 8, 16, 128), BF16),
-    "got_spectrum": pltpu.VMEM((3, NA, 8, 16, 128), BF16),
+    "acc_f": pltpu.VMEM((KB, 128), F32),
+    "swap_f": pltpu.VMEM((64, 128), F32),
+    "out_spectrum": pltpu.VMEM((6, NA, 64, 128), BF16),
+    "got_spectrum": pltpu.VMEM((6, NA, 64, 128), BF16),
     "table": pltpu.VMEM((10240, JH), BF16),
     "cosine": pltpu.VMEM((8, JH), F32),
     "up": pltpu.VMEM((4, 8, JH), F32),
@@ -541,19 +545,21 @@
     "lhs_u": pltpu.VMEM((256, 256), BF16),
     "acc_u": pltpu.VMEM((3, 256, 1536), F32),
     "load": pltpu.SemaphoreType.DMA((2,)),
-    "own": pltpu.SemaphoreType.DMA((5, 6)),
+    "own": pltpu.SemaphoreType.DMA((6, 6)),
     "r_send": pltpu.SemaphoreType.DMA((6, 16)),
     "r_recv": pltpu.SemaphoreType.DMA((6, 16)),
-    "s_send": pltpu.SemaphoreType.DMA((3, 16)),
-    "s_recv": pltpu.SemaphoreType.DMA((3, 16)),
+    "s_send": pltpu.SemaphoreType.DMA((6, 16)),
+    "s_recv": pltpu.SemaphoreType.DMA((6, 16)),
     "w_send": pltpu.SemaphoreType.DMA((16,)),
     "w_recv": pltpu.SemaphoreType.DMA((16,)),
     "c_send": pltpu.SemaphoreType.DMA((4, 16)),
     "c_recv": pltpu.SemaphoreType.DMA((4, 16)),
     "f_send": pltpu.SemaphoreType.DMA((4, 16)),
     "f_recv": pltpu.SemaphoreType.DMA((4, 16)),
-    "u_send": pltpu.SemaphoreType.DMA((4, 16)),
-    "u_recv": pltpu.SemaphoreType.DMA((4, 16)),
+    "u_send": pltpu.SemaphoreType.DMA((3, 16)),
+    "u_recv": pltpu.SemaphoreType.DMA((3, 16)),
+    "l_send": pltpu.SemaphoreType.DMA((3, 16)),
+    "l_recv": pltpu.SemaphoreType.DMA((3, 16)),
 }
 
 
@@ -598,19 +604,19 @@
 
     own_tail = pltpu.make_async_copy(v["out_tail"].at[lon], v["got_tail"].at[lon], own.at[0, 5])
 
-    def spectrum_copy(gp, d):
+    def spectrum_copy(g, d):
         return to_peer(
             "lat",
             d,
-            lambda peer: v["out_spectrum"].at[gp, peer],
-            v["got_spectrum"].at[gp, lat],
-            v["s_send"].at[gp, d],
-            v["s_recv"].at[gp, d],
-        )
-
-    def own_spectrum(gp):
+            lambda peer: v["out_spectrum"].at[g, peer],
+            v["got_spectrum"].at[g, lat],
+            v["s_send"].at[g, d],
+            v["s_recv"].at[g, d],
+        )
+
+    def own_spectrum(g):
         return pltpu.make_async_copy(
-            v["out_spectrum"].at[gp, lat], v["got_spectrum"].at[gp, lat], own.at[1, gp]
+            v["out_spectrum"].at[g, lat], v["got_spectrum"].at[g, lat], own.at[1, g]
         )
 
     def weight_copy(d):
@@ -654,6 +660,21 @@
             v["u_recv"].at[c, d],
         )
 
+    def last_copy(gp, d):
+        return to_peer(
+            "lat",
+            d,
+            lambda peer: v["out_u"].at[3, peer, gp],
+            v["got_u"].at[3, lat, gp],
+            v["l_send"].at[gp, d],
+            v["l_recv"].at[gp, d],
+        )
+
+    def own_last(gp):
+        return pltpu.make_async_copy(
+            v["out_u"].at[3, lat, gp], v["got_u"].at[3, lat, gp], own.at[5, gp]
+        )
+
     def own_u(c):
         return pltpu.make_async_copy(v["out_u"].at[c, lat], v["got_u"].at[c, lat], own.at[4, c])
 
@@ -667,23 +688,22 @@
             rows_copy(g, d).start()
         own_rows(g).start()
 
-    def dft_step(g, gg):
-        dft_half(g, gg, v["got_rows"], v["waves_f"], v["acc_f"])
-
     def got_rows(g):
         own_rows(g).wait()
         for d in OTHERS:
             rows_copy(g, d).wait_recv()
 
-    def send_spectrum(gp):
+    def transform(g):
+        dft(g, v["got_rows"], v["waves_f"], v["acc_f"])
+
         def one(d):
             peer = lax.rem(lat + d, 16)
-            dft_place(gp, peer, v["acc_f"], v["swap_f"], v["out_spectrum"])
-            spectrum_copy(gp, d).start()
+            dft_place(g, peer, v["acc_f"], v["swap_f"], v["out_spectrum"])
+            spectrum_copy(g, d).start()
 
         each(1, 16, one)
-        dft_place(gp, lat, v["acc_f"], v["swap_f"], v["out_spectrum"])
-        own_spectrum(gp).start()
+        dft_place(g, lat, v["acc_f"], v["swap_f"], v["out_spectrum"])
+        own_spectrum(g).start()
 
     load_points = pltpu.make_async_copy(points_any, v["points"], v["load"].at[0])
     load_points.start()
@@ -719,27 +739,25 @@
     def pair(gp):
         for gg in range(2):
             got_rows(2 * gp + gg)
-            dft_step(2 * gp + gg, gg)
-        send_spectrum(gp)
+            transform(2 * gp + gg)
         residual(gp, v["got_rows"], v["acc_u"])
 
     each(0, 2, pair)
     got_rows(4)
-    dft_step(4, 0)
+    transform(4)
     own_tail.wait()
     for d in OTHERS:
         tail_copy(d).wait_recv()
     each(0, NZ, lambda z: unpack_tail(z, v["got_tail"], v["got_rows"]))
-    dft_step(5, 1)
-    send_spectrum(2)
+    transform(5)
     residual(2, v["got_rows"], v["acc_u"])
 
-    def got_spectrum(gp):
-        own_spectrum(gp).wait()
-        for d in OTHERS:
-            spectrum_copy(gp, d).wait()
-
-    each(0, 3, got_spectrum)
+    def got_spectrum(g):
+        own_spectrum(g).wait()
+        for d in OTHERS:
+            spectrum_copy(g, d).wait()
+
+    each(0, 6, got_spectrum)
     for c in range(4):
         for mg in CHUNKS[c]:
             analyse(mg, v["got_spectrum"], v["table"], v["every"])
@@ -759,19 +777,16 @@
             mode_copy(c, "f", d).start()
         own_modes(c, "f").start()
 
-    def inverse_step(c, last):
+    def inverse(c, gp):
+        inverse_part(
+            c, gp, v["got_u"], v["waves_i"], v["wide_u"], v["rows_u"], v["lhs_u"], v["acc_u"]
+        )
+
+    def inverse_step(c):
         own_u(c).wait()
         for d in OTHERS:
             u_copy(c, d).wait()
-
-        def one(gp):
-            inverse_part(
-                c, gp, v["got_u"], v["waves_i"], v["wide_u"], v["rows_u"], v["lhs_u"], v["acc_u"]
-            )
-            if last:
-                emit(gp, v["acc_u"], o_ref)
-
-        each(0, 3, one)
+        each(0, 3, lambda gp: inverse(c, gp))
 
     for c in range(4):
         own_modes(c, "f").wait()
@@ -780,11 +795,20 @@
         each(0, NZ, lambda z, c=c: synthesis_rows(z, c, v["got_f"], v["every"]))
         for place in range(2):
             synthesise(c, place, v["table"], v["every"], v["out_u"])
-        for d in OTHERS:
-            u_copy(c, d).start()
-        own_u(c).start()
+        if c < 3:
+            for d in OTHERS:
+                u_copy(c, d).start()
+            own_u(c).start()
+        else:
+
+            def send_last(gp):
+                for d in OTHERS:
+                    last_copy(gp, d).start()
+                own_last(gp).start()
+
+            each(0, 3, send_last)
         if c >= 1:
-            inverse_step(c - 1, False)
+            inverse_step(c - 1)
 
     def rows_sent(g):
         for d in OTHERS:
@@ -793,7 +817,15 @@
     each(0, 5, rows_sent)
     for d in OTHERS:
         tail_copy(d).wait_send()
-    inverse_step(3, True)
+
+    def finish(gp):
+        own_last(gp).wait()
+        for d in OTHERS:
+            last_copy(gp, d).wait()
+        inverse(3, gp)
+        emit(gp, v["acc_u"], o_ref)
+
+    each(0, 3, finish)
 
 
 def on_device(grid, norm_gain, mlp_in, mlp_out, filter_weight):

time: 208 us -> 207 us (level)
  no operation moved by 1% of the time
where the time goes in v5:
time: 207 us
  Pallas kernels  203 us (98%)
  local copies, waits for them, and re-layouts  3.12 us (2%)
    pallas_call x1, Pallas kernels, on_device(): pl.pallas_call(block_kernel, out_shape=jax.ShapeDtypeStruct((JD, 16, NLON...  203 us

profile of v5, /device:TPU:1, one launch (start us, length us, event | category | flops | bytes accessed | tf_op | source)
XLA Modules:
  0.0 206.5 jit_solution(4778251408310057191)
XLA Ops:
  0.0 203.4 %shard_map.55 = bf16[45,16,1440]{2,1,0:T(8,128)(2,1)} custom-call(bf16[45,90,256]{2,1,0:T(8,128)(2,1)} %bitcast.4, f32[1,256]{1,0:T(1,128)} %bitcast.5, bf16[256,512]{1,0:T(8,128)(2,1)} %in_ref.1, bf16[512,256]{1,0:T(8,128)(2,1)} %out_ref.1, bf16[2,256,256]{2,1,0:T(8,128)(2,1)} %weight_any.1), custom_call_target="tpu_custom_call" | custom-call | flops 20000000000 | bytes 10000000 | tf_op jit(solution)/shard_map/pallas_call | solution.py:832
  203.4 3.1 %copy.7 = bf16[16,45,1440]{2,0,1:T(8,128)(2,1)} copy(bf16[16,45,1440]{2,0,1:T(8,128)(2,1)} %bitcast.3) | data formatting | bytes 4147200

commit v6 on v5

--- a/solution.py
+++ b/solution.py
@@ -212,18 +212,16 @@
         put_basis(4 + 2 * c, o_ref, multiple, points, 2.0)
 
 
-def dft(g, x_ref, table_ref, acc_ref):
+def dft_part(g, part, x_ref, table_ref, acc_ref):
     lat = lax.axis_index("lat")
     band = jnp.minimum(lat, 15 - lat)
     local = lax.broadcasted_iota(jnp.int32, (8, 128), 1) // 16 + 8 * g
     theta = jnp.pi * ((local + band * JD).astype(F32) + 0.5) / NLAT
     weights = jnp.pi / NLAT * jnp.sin(theta) / NLON
     weights = jnp.where(local < JD, weights, 0.0)[:1]
+    rows = pl.ds(pl.multiple_of(part * 256, 256), 256)
     x = x_ref[g].reshape(NZ * NP, 128)
-    for part in range(4):
-        rows = slice(part * 256, (part + 1) * 256)
-        acc = jnp.dot(table_ref[rows, :], x, preferred_element_type=F32)
-        acc_ref[rows, :] = acc * weights
+    acc_ref[rows, :] = jnp.dot(table_ref[rows, :], x, preferred_element_type=F32) * weights
 
 
 def dft_place(g, a, acc_ref, swap_ref, o_ref):
@@ -499,11 +497,8 @@
 
 
 def emit(gp, acc_ref, o_ref):
-    for j in range(16):
-
-        @pl.when(16 * gp + j < JD)
-        def _(j=j):
-            o_ref[band_row(16 * gp + j)] = acc_ref[gp, 16 * j : 16 * j + 16, :NLON].astype(BF16)
+    for j in range(min(16, JD - 16 * gp)):
+        o_ref[band_row(16 * gp + j)] = acc_ref[gp, 16 * j : 16 * j + 16, :NLON].astype(BF16)
 
 
 VM = pl.BlockSpec(memory_space=pltpu.VMEM)
@@ -544,7 +539,9 @@
     "rows_u": pltpu.VMEM((2, 256, 128), F32),
     "lhs_u": pltpu.VMEM((256, 256), BF16),
     "acc_u": pltpu.VMEM((3, 256, 1536), F32),
+    "updated": pltpu.VMEM((JD, 16, NLON), BF16),
     "load": pltpu.SemaphoreType.DMA((2,)),
+    "store": pltpu.SemaphoreType.DMA((3,)),
     "own": pltpu.SemaphoreType.DMA((6, 6)),
     "r_send": pltpu.SemaphoreType.DMA((6, 16)),
     "r_recv": pltpu.SemaphoreType.DMA((6, 16)),
@@ -571,7 +568,7 @@
     lax.fori_loop(low, high, step, 0)
 
 
-def block_kernel(points_any, gain_ref, in_ref, out_ref, weight_any, o_ref, *scratch):
+def block_kernel(points_any, gain_ref, in_ref, out_ref, weight_any, o_any, *scratch):
     v = dict(zip(SCRATCH, scratch))
     lat = lax.axis_index("lat")
     lon = lax.axis_index("lon")
@@ -694,15 +691,18 @@
             rows_copy(g, d).wait_recv()
 
     def transform(g):
-        dft(g, v["got_rows"], v["waves_f"], v["acc_f"])
-
-        def one(d):
-            peer = lax.rem(lat + d, 16)
-            dft_place(g, peer, v["acc_f"], v["swap_f"], v["out_spectrum"])
-            spectrum_copy(g, d).start()
-
-        each(1, 16, one)
-        dft_place(g, lat, v["acc_f"], v["swap_f"], v["out_spectrum"])
+        def part(k):
+            quarter = lax.rem(lat // 4 + k, 4)
+            dft_part(g, quarter, v["got_rows"], v["waves_f"], v["acc_f"])
+            for i in range(4):
+                peer = 4 * quarter + i
+                dft_place(g, peer, v["acc_f"], v["swap_f"], v["out_spectrum"])
+
+                @pl.when(peer != lat)
+                def _():
+                    spectrum_copy(g, lax.rem(peer - lat + 16, 16)).start()
+
+        each(0, 4, part)
         own_spectrum(g).start()
 
     load_points = pltpu.make_async_copy(points_any, v["points"], v["load"].at[0])
@@ -713,6 +713,9 @@
     mlp_step(0)
     pl.semaphore_wait(barrier, 30)
     send_rows(0)
+    for d in OTHERS:
+        weight_copy(d).start()
+    own_weight.start()
 
     def mlp_more(g):
         mlp_step(g)
@@ -726,10 +729,6 @@
     for d in OTHERS:
         tail_copy(d).start()
     own_tail.start()
-    for d in OTHERS:
-        weight_copy(d).start()
-    own_weight.start()
-
     forward_basis(v["basis_f"])
     forward_waves(v["basis_f"], v["waves_f"])
     legendre(v["cosine"], v["table"], v["up"], v["low"], v["scale"], v["swap_l"])
@@ -818,14 +817,21 @@
     for d in OTHERS:
         tail_copy(d).wait_send()
 
-    def finish(gp):
+    stores = []
+    for gp in range(3):
         own_last(gp).wait()
         for d in OTHERS:
             last_copy(gp, d).wait()
         inverse(3, gp)
-        emit(gp, v["acc_u"], o_ref)
-
-    each(0, 3, finish)
+        emit(gp, v["acc_u"], v["updated"])
+        count = min(16, JD - 16 * gp)
+        part = pl.ds(jnp.where(lat >= 8, JD - 16 * gp - count, 16 * gp), count)
+        stores.append(
+            pltpu.make_async_copy(v["updated"].at[part], o_any.at[part], v["store"].at[gp])
+        )
+        stores[gp].start()
+    for store in stores:
+        store.wait()
 
 
 def on_device(grid, norm_gain, mlp_in, mlp_out, filter_weight):
@@ -833,7 +839,7 @@
         block_kernel,
         out_shape=jax.ShapeDtypeStruct((JD, 16, NLON), BF16),
         in_specs=[ANY, VM, VM, VM, ANY],
-        out_specs=VM,
+        out_specs=ANY,
         scratch_shapes=list(SCRATCH.values()),
         cost_estimate=pl.CostEstimate(
             flops=20_000_000_000, bytes_accessed=10_000_000, transcendentals=0

time: 207 us -> 206 us (level)
  no operation moved by 1% of the time
where the time goes in v6:
time: 206 us
  Pallas kernels  203 us (99%)
  local copies, waits for them, and re-layouts  3.12 us (2%)
    pallas_call x1, Pallas kernels, on_device(): pl.pallas_call(block_kernel, out_shape=jax.ShapeDtypeStruct((JD, 16, NLON...  203 us

profile of v6, /device:TPU:1, one launch (start us, length us, event | category | flops | bytes accessed | tf_op | source)
XLA Modules:
  0.0 206.3 jit_solution(18320280020468413398)
XLA Ops:
  0.0 203.1 %shard_map.55 = bf16[45,16,1440]{2,1,0:T(8,128)(2,1)} custom-call(bf16[45,90,256]{2,1,0:T(8,128)(2,1)} %bitcast.4, f32[1,256]{1,0:T(1,128)} %bitcast.5, bf16[256,512]{1,0:T(8,128)(2,1)} %in_ref.1, bf16[512,256]{1,0:T(8,128)(2,1)} %out_ref.1, bf16[2,256,256]{2,1,0:T(8,128)(2,1)} %weight_any.1), custom_call_target="tpu_custom_call" | custom-call | flops 20000000000 | bytes 10000000 | tf_op jit(solution)/shard_map/pallas_call | solution.py:838
  203.2 3.1 %copy.7 = bf16[16,45,1440]{2,0,1:T(8,128)(2,1)} copy(bf16[16,45,1440]{2,0,1:T(8,128)(2,1)} %bitcast.3) | data formatting | bytes 4147200
